TPU v7x, 128 devices: a whole 4x4x4 slice. The times are simulated.
128 devices in a mesh: wide: 32 (over x, y, core), narrow: 4 (over z).
Axes of the slice: x: 4, y: 4, z: 4, core: 2. Of those that a mesh axis runs over, the one named last changes fastest.
Arguments:
- right_side: float32 [512, 128, 512], P('wide', 'narrow'), may hold values from -18 to 18
- coef_fine: float32 [2, 512, 128, 512], P(None, 'wide', 'narrow'), may hold values from 0.05 to 1
- coef_mid: float32 [2, 256, 64, 256], P(None, 'wide', 'narrow'), may hold values from 0.05 to 1
- coef_low: float32 [2, 128, 32, 128], P(None, 'wide', 'narrow'), may hold values from 0.05 to 1
- coarse_offset: int32 [1], replicated, may hold values from 1 to 31
Outputs:
- correction: float32 [512, 128, 512], P('wide', 'narrow')
- remainder: float32 [512, 128, 512], P('wide', 'narrow')
All inputs are finite; a program needn't handle non-finite values.
Results may differ from a plain program's by a relative error of at most 0.0003.
Values sent between devices are 32-bit elements; how exact they have to be, the bound alone decides.
A program may use at most 256 MiB of HBM per device.

v0:
```python
from functools import partial

import jax
import jax.numpy as jnp
from jax import lax
from jax.sharding import PartitionSpec as P

NU = 2
NUC = 6


def with_halo(block, sides, width):
    for axis, dim in sides:
        count = lax.axis_size(axis)
        forward = [(i, i + 1) for i in range(count - 1)]
        forward.append((count - 1, 0))
        backward = [(target, source) for source, target in forward]
        low = lax.ppermute(
            lax.slice_in_dim(block, block.shape[dim] - width, None, axis=dim), axis, forward
        )
        high = lax.ppermute(lax.slice_in_dim(block, 0, width, axis=dim), axis, backward)
        block = jnp.concatenate([low, block, high], axis=dim)
    return block


def from_behind(x, axis, by):
    devices = lax.axis_size(axis)
    return lax.ppermute(x, axis, [(i, (i + by) % devices) for i in range(devices)])


def neighbours(padded):
    return (
        padded[:-2, 1:-1, 1:-1],
        padded[2:, 1:-1, 1:-1],
        padded[1:-1, :-2, 1:-1],
        padded[1:-1, 2:, 1:-1],
        padded[1:-1, 1:-1, :-2],
        padded[1:-1, 1:-1, 2:],
    )


def face_terms(coef_pad, diag_term):
    centre = coef_pad[1:-1, 1:-1, 1:-1]
    face_list = [0.5 * (centre + beside_all) for beside_all in neighbours(coef_pad)]
    face_total = face_list[0]
    for other in face_list[1:]:
        face_total = face_total + other
    return (face_list, face_total + diag_term)


def pulled(face_list, iterate_pad):
    beside_all = neighbours(iterate_pad)
    summed = face_list[0] * beside_all[0]
    for place in range(1, 6):
        summed = summed + face_list[place] * beside_all[place]
    return summed


def checker(shape):
    plane_x = lax.broadcasted_iota(jnp.int32, shape, 0)
    plane_y = lax.broadcasted_iota(jnp.int32, shape, 1)
    plane_z = lax.broadcasted_iota(jnp.int32, shape, 2)
    return (plane_x + plane_y + plane_z) % 2 == 0


def relaxed(iterate, iterate_pad, source, face_list, diagonal, even_cells, colour):
    updated = (source + pulled(face_list, iterate_pad)) / diagonal
    chosen = even_cells if colour == 0 else jnp.logical_not(even_cells)
    return jnp.where(chosen, updated, iterate)


def restrict(residue):
    extent_x, extent_y, extent_z = residue.shape
    blocks = residue.reshape(extent_x // 2, 2, extent_y // 2, 2, extent_z // 2, 2)
    return 0.5 * blocks.sum(axis=(1, 3, 5))


def prolong(coarse):
    extent_x, extent_y, extent_z = coarse.shape
    spread_out = jnp.broadcast_to(
        coarse[:, None, :, None, :, None], (extent_x, 2, extent_y, 2, extent_z, 2)
    )
    return spread_out.reshape(2 * extent_x, 2 * extent_y, 2 * extent_z)


def smooth(iterate, source, face_list, diagonal, repeats, zero_start, grower):
    even_cells = checker(iterate.shape)
    for repeat in range(repeats):
        for colour in (0, 1):
            if zero_start and repeat == 0 and (colour == 0):
                iterate_pad = jnp.pad(iterate, 1)
            else:
                iterate_pad = grower(iterate)
            iterate = relaxed(iterate, iterate_pad, source, face_list, diagonal, even_cells, colour)
    return iterate


def residual(iterate, source, face_list, diagonal, grower):
    return source - (diagonal * iterate - pulled(face_list, grower(iterate)))


def on_device(right_side, coef_fine, coef_mid, coef_low, coarse_offset):
    wide_count = lax.axis_size("wide")
    narrow_count = lax.axis_size("narrow")
    wide_here = lax.axis_index("wide")
    narrow_here = lax.axis_index("narrow")
    box_offset = coarse_offset[0]
    wide_bits = wide_count.bit_length() - 1

    def extend(field_data, wide_box):
        padded = with_halo(field_data, (("wide", 0), ("narrow", 1)), 1)
        row_index = lax.broadcasted_iota(jnp.int32, padded.shape, 0)
        col_index = lax.broadcasted_iota(jnp.int32, padded.shape, 1)
        last_row = padded.shape[0] - 1
        last_col = padded.shape[1] - 1
        outside = (row_index == 0) & (wide_box == 0) | (row_index == last_row) & (
            wide_box == wide_count - 1
        )
        outside = (
            outside
            | (col_index == 0) & (narrow_here == 0)
            | (col_index == last_col) & (narrow_here == narrow_count - 1)
        )
        padded = jnp.where(outside, jnp.zeros_like(padded), padded)
        return jnp.pad(padded, ((0, 0), (0, 0), (1, 1)))

    grow_fine = partial(extend, wide_box=wide_here)
    fine_faces, fine_diag = face_terms(grow_fine(coef_fine[0]), coef_fine[1])
    fine_field = smooth(
        jnp.zeros_like(right_side), right_side, fine_faces, fine_diag, NU, True, grow_fine
    )
    mid_source = restrict(residual(fine_field, right_side, fine_faces, fine_diag, grow_fine))
    carried = mid_source
    for bit_place in range(wide_bits):
        arrived = from_behind(carried, "wide", 1 << bit_place)
        carried = jnp.where(box_offset // (1 << bit_place) % 2 == 1, arrived, carried)
    owned_box = (wide_here - box_offset) % wide_count
    grow_mid = partial(extend, wide_box=owned_box)
    mid_faces, mid_diag = face_terms(grow_mid(coef_mid[0]), coef_mid[1])
    mid_field = smooth(jnp.zeros_like(carried), carried, mid_faces, mid_diag, NU, True, grow_mid)
    low_source = restrict(residual(mid_field, carried, mid_faces, mid_diag, grow_mid))
    low_faces, low_diag = face_terms(grow_mid(coef_low[0]), coef_low[1])
    low_field = smooth(
        jnp.zeros_like(low_source), low_source, low_faces, low_diag, NUC, True, grow_mid
    )
    mid_field = mid_field + prolong(low_field)
    correction_mid = smooth(mid_field, carried, mid_faces, mid_diag, NU, False, grow_mid)
    for bit_place in range(wide_bits):
        returned = from_behind(correction_mid, "wide", -(1 << bit_place))
        correction_mid = jnp.where(
            box_offset // (1 << bit_place) % 2 == 1, returned, correction_mid
        )
    fine_field = fine_field + prolong(correction_mid)
    fine_field = smooth(fine_field, right_side, fine_faces, fine_diag, NU, False, grow_fine)
    remainder = residual(fine_field, right_side, fine_faces, fine_diag, grow_fine)
    return (fine_field, remainder)


def solution(mesh):
    return jax.shard_map(
        on_device,
        mesh=mesh,
        in_specs=(
            P("wide", "narrow", None),
            P(None, "wide", "narrow", None),
            P(None, "wide", "narrow", None),
            P(None, "wide", "narrow", None),
            P(),
        ),
        out_specs=(P("wide", "narrow", None), P("wide", "narrow", None)),
        check_vma=False,
    )
```

profile of v0, /device:TPU:0, one launch (start us, length us, event | category | flops | bytes accessed | tf_op | source)
XLA Modules:
  0.0 674.1 jit_solution(9831380762682163718)
XLA Ops:
  1.6 5.1 collective-permute-start.1
  16.7 3.0 fusion.111
  19.9 5.1 collective-permute-start.5
  33.2 3.4 fusion.11
  36.7 5.1 collective-permute-start.9
  49.8 2.3 fusion.18
  52.3 5.1 collective-permute-start.13
  65.4 2.3 fusion.25
  67.8 5.1 collective-permute-start.17
  80.6 2.8 fusion.31
  83.5 69.1 %reshape.24 = f32[8,2,16,2,256,2]{5,4,3,2,1,0:T(8,128)} reshape(f32[16,32,512]{2,1,0:T(8,128)} %fusion.31) | data formatting | bytes 2097152 | tf_op jit(solution)/shard_map/reshape | solution.py:74
  152.6 20.8 %reduce_sum.18 = f32[8,16,256]{2,1,0:T(8,128)S(1)} reduce(f32[8,2,16,2,256,2]{5,4,3,2,1,0:T(8,128)} %reshape.24, f32[]{:T(128)} %constant.172.clone.1), dimensions={1,3,5}, to_apply=%region_0.1 | reduce | flops 229376 | bytes 1179652 | tf_op jit(solution)/shard_map/reduce_sum | solution.py:75
  174.8 7.4 %collective-permute-done.20 = f32[8,16,256]{2,1,0:T(8,128)} collective-permute-done((f32[8,16,256]{2,1,0:T(8,128)}, f32[8,16,256]{2,1,0:T(8,128)}, u32[]{:S(2)}, u32[]{:S(2)}) %collective-permute-start.20) | collective-permute-done | bytes 131104 | tf_op jit(solution)/shard_map/ppermute | solution.py:28
  183.5 5.1 collective-permute-start.26
  188.5 3.4 collective-permute-done.21
  193.3 8.2 %collective-permute-done.22 = f32[8,16,256]{2,1,0:T(8,128)} collective-permute-done((f32[8,16,256]{2,1,0:T(8,128)}, f32[8,16,256]{2,1,0:T(8,128)}, u32[]{:S(2)}, u32[]{:S(2)}) %collective-permute-start.22) | collective-permute-done | bytes 131104 | tf_op jit(solution)/shard_map/ppermute | solution.py:28
  210.0 5.2 collective-permute-done.24
  216.7 5.1 collective-permute-start.30
  229.3 5.1 collective-permute-start.34
  234.4 5.1 collective-permute-start.46
  245.2 5.1 collective-permute-start.38
  257.2 5.1 collective-permute-start.42
  265.8 3.2 collective-permute-start.44
  271.6 10.4 %reshape.25 = f32[4,2,8,2,128,2]{5,4,3,2,1,0:T(8,128)} reshape(f32[8,16,256]{2,1,0:T(8,128)} %fusion.143) | data formatting | bytes 262144 | tf_op jit(solution)/shard_map/reshape | solution.py:74
  282.0 4.0 reduce_sum.19
  287.3 5.1 collective-permute-start.50
  294.3 2.8 collective-permute-start.52
  300.2 5.4 collective-permute-start.54
  313.7 5.1 collective-permute-start.58
  327.4 5.1 collective-permute-start.62
  339.7 5.1 collective-permute-start.66
  352.0 5.1 collective-permute-start.70
  364.3 5.1 collective-permute-start.74
  377.3 5.1 collective-permute-start.78
  389.6 5.1 collective-permute-start.82
  402.0 5.1 collective-permute-start.86
  414.3 5.1 collective-permute-start.90
  427.2 3.9 broadcast_in_dim.24
  431.1 7.5 %reshape.26 = f32[8,16,256]{2,1,0:T(8,128)} reshape(f32[4,2,8,2,128,2]{5,4,3,2,1,0:T(8,128)} %broadcast_in_dim.24) | data formatting | bytes 262144 | tf_op jit(solution)/shard_map/reshape | solution.py:83
  439.6 5.1 collective-permute-start.94
  452.9 5.1 collective-permute-start.98
  459.4 3.2 collective-permute-start.100
  464.0 3.5 collective-permute-done.99
  467.9 5.1 collective-permute-start.102
  474.5 3.2 collective-permute-start.104
  479.8 5.1 collective-permute-start.106
  486.4 3.5 collective-permute-start.108
  491.6 4.3 collective-permute-start.109
  495.8 2.5 collective-permute-done.109
  498.5 5.0 collective-permute-done.110
  503.5 6.5 collective-permute-done.111
  510.1 5.2 collective-permute-done.112
  515.4 7.8 %collective-permute-done.113 = f32[8,16,256]{2,1,0:T(8,128)S(1)} collective-permute-done((f32[8,16,256]{2,1,0:T(8,128)S(1)}, f32[8,16,256]{2,1,0:T(8,128)S(1)}, u32[]{:S(2)}, u32[]{:S(2)}) %collective-permute-start.113) | collective-permute-done | bytes 131104 | tf_op jit(solution)/shard_map/ppermute | solution.py:28
  523.2 21.4 %broadcast_in_dim.25 = f32[8,2,16,2,256,2]{5,4,3,2,1,0:T(8,128)} broadcast(f32[8,16,256]{2,1,0:T(8,128)S(1)} %broadcast_select_fusion.8), dimensions={0,2,4} | broadcast | bytes 1179648 | tf_op jit(solution)/shard_map/broadcast_in_dim | solution.py:80
  544.6 47.2 %reshape.27 = f32[16,32,512]{2,1,0:T(8,128)} reshape(f32[8,2,16,2,256,2]{5,4,3,2,1,0:T(8,128)} %broadcast_in_dim.25) | data formatting | bytes 2097152 | tf_op jit(solution)/shard_map/reshape | solution.py:83
  594.1 7.2 %collective-permute-start.115 = (f32[1,32,512]{2,1,0:T(8,128)S(1)}, f32[1,32,512]{2,1,0:T(8,128)S(1)}, u32[]{:S(2)}, u32[]{:S(2)}) collective-permute-start(f32[1,32,512]{2,1,0:T(8,128)S(1)} %get-tuple-element.55), channel_id=1, source_target_pairs={{4,0},{8,4},{12,8},{16,12},{20,16},{24,20},{28,24},{32,28},{36,32}... | collective-permute-start | bytes 196616 | tf_op jit(solution)/shard_map/ppermute | solution.py:21
  609.0 2.3 fusion.38
  611.4 5.1 collective-permute-start.119
  624.7 2.3 fusion.45
  627.1 5.1 collective-permute-start.123
  642.8 5.1 collective-permute-start.127
  655.6 2.3 fusion.59
  658.1 5.1 collective-permute-start.131
  670.8 2.8 fusion.65
  (448 shorter events, 228.7 us)
Async XLA Ops:
  1.5 7.1 %collective-permute-start = (f32[1,32,512]{2,1,0:T(8,128)S(1)}, f32[1,32,512]{2,1,0:T(8,128)S(1)}, u32[]{:S(2)}, u32[]{:S(2)}) collective-permute-start(f32[1,32,512]{2,1,0:T(8,128)S(1)} %get-tuple-element.24), channel_id=1, source_target_pairs={{0,4},{4,8},{8,12},{12,16},{16,20},{20,24},{24,28},{28,32},{32,36}... | collective-permute-start | bytes 196616 | tf_op jit(solution)/shard_map/ppermute | solution.py:18
  1.6 7.0 %collective-permute-start.1 = (f32[1,32,512]{2,1,0:T(8,128)S(1)}, f32[1,32,512]{2,1,0:T(8,128)S(1)}, u32[]{:S(2)}, u32[]{:S(2)}) collective-permute-start(f32[1,32,512]{2,1,0:T(8,128)S(1)} %get-tuple-element.25), channel_id=1, source_target_pairs={{4,0},{8,4},{12,8},{16,12},{20,16},{24,20},{28,24},{32,28},{36,32}... | collective-permute-start | bytes 196616 | tf_op jit(solution)/shard_map/ppermute | solution.py:21
  19.8 7.1 %collective-permute-start.4 = (f32[1,32,512]{2,1,0:T(8,128)S(1)}, f32[1,32,512]{2,1,0:T(8,128)S(1)}, u32[]{:S(2)}, u32[]{:S(2)}) collective-permute-start(f32[1,32,512]{2,1,0:T(8,128)S(1)} %get-tuple-element.62), channel_id=1, source_target_pairs={{0,4},{4,8},{8,12},{12,16},{16,20},{20,24},{24,28},{28,32},{32,36}... | collective-permute-start | bytes 196616 | tf_op jit(solution)/shard_map/ppermute | solution.py:18
  19.9 7.0 %collective-permute-start.5 = (f32[1,32,512]{2,1,0:T(8,128)S(1)}, f32[1,32,512]{2,1,0:T(8,128)S(1)}, u32[]{:S(2)}, u32[]{:S(2)}) collective-permute-start(f32[1,32,512]{2,1,0:T(8,128)S(1)} %get-tuple-element.63), channel_id=1, source_target_pairs={{4,0},{8,4},{12,8},{16,12},{20,16},{24,20},{28,24},{32,28},{36,32}... | collective-permute-start | bytes 196616 | tf_op jit(solution)/shard_map/ppermute | solution.py:21
  36.6 7.1 %collective-permute-start.8 = (f32[1,32,512]{2,1,0:T(8,128)S(1)}, f32[1,32,512]{2,1,0:T(8,128)S(1)}, u32[]{:S(2)}, u32[]{:S(2)}) collective-permute-start(f32[1,32,512]{2,1,0:T(8,128)S(1)} %get-tuple-element.60), channel_id=1, source_target_pairs={{0,4},{4,8},{8,12},{12,16},{16,20},{20,24},{24,28},{28,32},{32,36}... | collective-permute-start | bytes 196616 | tf_op jit(solution)/shard_map/ppermute | solution.py:18
  36.7 7.0 %collective-permute-start.9 = (f32[1,32,512]{2,1,0:T(8,128)S(1)}, f32[1,32,512]{2,1,0:T(8,128)S(1)}, u32[]{:S(2)}, u32[]{:S(2)}) collective-permute-start(f32[1,32,512]{2,1,0:T(8,128)S(1)} %get-tuple-element.61), channel_id=1, source_target_pairs={{4,0},{8,4},{12,8},{16,12},{20,16},{24,20},{28,24},{32,28},{36,32}... | collective-permute-start | bytes 196616 | tf_op jit(solution)/shard_map/ppermute | solution.py:21
  52.2 7.1 %collective-permute-start.12 = (f32[1,32,512]{2,1,0:T(8,128)S(1)}, f32[1,32,512]{2,1,0:T(8,128)S(1)}, u32[]{:S(2)}, u32[]{:S(2)}) collective-permute-start(f32[1,32,512]{2,1,0:T(8,128)S(1)} %get-tuple-element.58), channel_id=1, source_target_pairs={{0,4},{4,8},{8,12},{12,16},{16,20},{20,24},{24,28},{28,32},{32,36}... | collective-permute-start | bytes 196616 | tf_op jit(solution)/shard_map/ppermute | solution.py:18
  52.3 7.0 %collective-permute-start.13 = (f32[1,32,512]{2,1,0:T(8,128)S(1)}, f32[1,32,512]{2,1,0:T(8,128)S(1)}, u32[]{:S(2)}, u32[]{:S(2)}) collective-permute-start(f32[1,32,512]{2,1,0:T(8,128)S(1)} %get-tuple-element.59), channel_id=1, source_target_pairs={{4,0},{8,4},{12,8},{16,12},{20,16},{24,20},{28,24},{32,28},{36,32}... | collective-permute-start | bytes 196616 | tf_op jit(solution)/shard_map/ppermute | solution.py:21
  67.7 7.1 %collective-permute-start.16 = (f32[1,32,512]{2,1,0:T(8,128)S(1)}, f32[1,32,512]{2,1,0:T(8,128)S(1)}, u32[]{:S(2)}, u32[]{:S(2)}) collective-permute-start(f32[1,32,512]{2,1,0:T(8,128)S(1)} %get-tuple-element.56), channel_id=1, source_target_pairs={{0,4},{4,8},{8,12},{12,16},{16,20},{20,24},{24,28},{28,32},{32,36}... | collective-permute-start | bytes 196616 | tf_op jit(solution)/shard_map/ppermute | solution.py:18
  67.8 7.0 %collective-permute-start.17 = (f32[1,32,512]{2,1,0:T(8,128)S(1)}, f32[1,32,512]{2,1,0:T(8,128)S(1)}, u32[]{:S(2)}, u32[]{:S(2)}) collective-permute-start(f32[1,32,512]{2,1,0:T(8,128)S(1)} %get-tuple-element.57), channel_id=1, source_target_pairs={{4,0},{8,4},{12,8},{16,12},{20,16},{24,20},{28,24},{32,28},{36,32}... | collective-permute-start | bytes 196616 | tf_op jit(solution)/shard_map/ppermute | solution.py:21
  174.1 8.0 %collective-permute-start.20 = (f32[8,16,256]{2,1,0:T(8,128)}, f32[8,16,256]{2,1,0:T(8,128)}, u32[]{:S(2)}, u32[]{:S(2)}) collective-permute-start(f32[8,16,256]{2,1,0:T(8,128)} %broadcast_multiply_fusion), channel_id=1, source_target_pairs={{0,4},{4,8},{8,12},{12,16},{16,20},{20,24},{24,28},{28,32},{32,36}... | collective-permute-start | bytes 393224 | tf_op jit(solution)/shard_map/ppermute | solution.py:28
  182.8 9.1 %collective-permute-start.21 = (f32[8,16,256]{2,1,0:T(8,128)}, f32[8,16,256]{2,1,0:T(8,128)S(1)}, u32[]{:S(2)}, u32[]{:S(2)}) collective-permute-start(f32[8,16,256]{2,1,0:T(8,128)} %broadcast_select_fusion.1), channel_id=1, source_target_pairs={{0,8},{4,12},{8,16},{12,20},{16,24},{20,28},{24,32},{28,36},{32,40... | collective-permute-start | bytes 393224 | tf_op jit(solution)/shard_map/ppermute | solution.py:28
  183.5 19.6 %collective-permute-start.25 = (f32[1,16,256]{2,1,0:T(8,128)}, f32[1,16,256]{2,1,0:T(8,128)S(1)}, u32[]{:S(2)}, u32[]{:S(2)}) collective-permute-start(f32[1,16,256]{2,1,0:T(8,128)} %get-tuple-element.64), channel_id=1, source_target_pairs={{0,4},{4,8},{8,12},{12,16},{16,20},{20,24},{24,28},{28,32},{32,36}... | collective-permute-start | bytes 49160 | tf_op jit(solution)/shard_map/ppermute | solution.py:18
  183.5 19.6 %collective-permute-start.26 = (f32[1,16,256]{2,1,0:T(8,128)}, f32[1,16,256]{2,1,0:T(8,128)}, u32[]{:S(2)}, u32[]{:S(2)}) collective-permute-start(f32[1,16,256]{2,1,0:T(8,128)} %get-tuple-element.65), channel_id=1, source_target_pairs={{4,0},{8,4},{12,8},{16,12},{20,16},{24,20},{28,24},{32,28},{36,32}... | collective-permute-start | bytes 49160 | tf_op jit(solution)/shard_map/ppermute | solution.py:21
  192.6 8.9 %collective-permute-start.22 = (f32[8,16,256]{2,1,0:T(8,128)}, f32[8,16,256]{2,1,0:T(8,128)}, u32[]{:S(2)}, u32[]{:S(2)}) collective-permute-start(f32[8,16,256]{2,1,0:T(8,128)} %broadcast_select_fusion.3), channel_id=1, source_target_pairs={{0,16},{4,20},{8,24},{12,28},{16,32},{20,36},{24,40},{28,44},{32,4... | collective-permute-start | bytes 393224 | tf_op jit(solution)/shard_map/ppermute | solution.py:28
  208.7 6.6 collective-permute-start.24
  216.6 6.6 collective-permute-start.29
  216.7 6.5 collective-permute-start.30
  229.2 10.2 %collective-permute-start.33 = (f32[1,16,256]{2,1,0:T(8,128)S(1)}, f32[1,16,256]{2,1,0:T(8,128)S(1)}, u32[]{:S(2)}, u32[]{:S(2)}) collective-permute-start(f32[1,16,256]{2,1,0:T(8,128)S(1)} %get-tuple-element.96), channel_id=1, source_target_pairs={{0,4},{4,8},{8,12},{12,16},{16,20},{20,24},{24,28},{28,32},{32,36}... | collective-permute-start | bytes 49160 | tf_op jit(solution)/shard_map/ppermute | solution.py:18
  229.3 10.1 %collective-permute-start.34 = (f32[1,16,256]{2,1,0:T(8,128)S(1)}, f32[1,16,256]{2,1,0:T(8,128)S(1)}, u32[]{:S(2)}, u32[]{:S(2)}) collective-permute-start(f32[1,16,256]{2,1,0:T(8,128)S(1)} %get-tuple-element.97), channel_id=1, source_target_pairs={{4,0},{8,4},{12,8},{16,12},{20,16},{24,20},{28,24},{32,28},{36,32}... | collective-permute-start | bytes 49160 | tf_op jit(solution)/shard_map/ppermute | solution.py:21
  234.4 27.9 %collective-permute-start.45 = (f32[1,8,128]{2,1,0:T(8,128)S(1)}, f32[1,8,128]{2,1,0:T(8,128)S(1)}, u32[]{:S(2)}, u32[]{:S(2)}) collective-permute-start(f32[1,8,128]{2,1,0:T(8,128)S(1)} %get-tuple-element.100), channel_id=1, source_target_pairs={{0,4},{4,8},{8,12},{12,16},{16,20},{20,24},{24,28},{28,32},{32,36}... | collective-permute-start | bytes 12296 | tf_op jit(solution)/shard_map/ppermute | solution.py:18
  234.4 27.9 %collective-permute-start.46 = (f32[1,8,128]{2,1,0:T(8,128)S(1)}, f32[1,8,128]{2,1,0:T(8,128)S(1)}, u32[]{:S(2)}, u32[]{:S(2)}) collective-permute-start(f32[1,8,128]{2,1,0:T(8,128)S(1)} %get-tuple-element.101), channel_id=1, source_target_pairs={{4,0},{8,4},{12,8},{16,12},{20,16},{24,20},{28,24},{32,28},{36,32}... | collective-permute-start | bytes 12296 | tf_op jit(solution)/shard_map/ppermute | solution.py:21
  245.2 6.6 collective-permute-start.37
  245.2 6.5 collective-permute-start.38
  257.1 8.5 %collective-permute-start.41 = (f32[1,16,256]{2,1,0:T(8,128)S(1)}, f32[1,16,256]{2,1,0:T(8,128)S(1)}, u32[]{:S(2)}, u32[]{:S(2)}) collective-permute-start(f32[1,16,256]{2,1,0:T(8,128)S(1)} %get-tuple-element.92), channel_id=1, source_target_pairs={{0,4},{4,8},{8,12},{12,16},{16,20},{20,24},{24,28},{28,32},{32,36}... | collective-permute-start | bytes 49160 | tf_op jit(solution)/shard_map/ppermute | solution.py:18
  257.2 8.4 %collective-permute-start.42 = (f32[1,16,256]{2,1,0:T(8,128)S(1)}, f32[1,16,256]{2,1,0:T(8,128)S(1)}, u32[]{:S(2)}, u32[]{:S(2)}) collective-permute-start(f32[1,16,256]{2,1,0:T(8,128)S(1)} %get-tuple-element.93), channel_id=1, source_target_pairs={{4,0},{8,4},{12,8},{16,12},{20,16},{24,20},{28,24},{32,28},{36,32}... | collective-permute-start | bytes 49160 | tf_op jit(solution)/shard_map/ppermute | solution.py:21
  262.3 6.6 collective-permute-start.47
  287.3 6.4 collective-permute-start.49
  287.3 6.4 collective-permute-start.50
  300.2 6.4 collective-permute-start.53
  300.2 6.8 %collective-permute-start.54 = (f32[1,8,128]{2,1,0:T(8,128)S(1)}, f32[1,8,128]{2,1,0:T(8,128)S(1)}, u32[]{:S(2)}, u32[]{:S(2)}) collective-permute-start(f32[1,8,128]{2,1,0:T(8,128)S(1)} %get-tuple-element.145), channel_id=1, source_target_pairs={{4,0},{8,4},{12,8},{16,12},{20,16},{24,20},{28,24},{32,28},{36,32}... | collective-permute-start | bytes 12296 | tf_op jit(solution)/shard_map/ppermute | solution.py:21
  313.6 6.4 collective-permute-start.57
  313.7 6.4 collective-permute-start.58
  327.3 6.4 collective-permute-start.61
  327.4 6.4 collective-permute-start.62
  339.6 6.4 collective-permute-start.65
  339.7 6.4 collective-permute-start.66
  351.9 6.4 collective-permute-start.69
  364.2 6.4 collective-permute-start.73
  377.2 6.4 collective-permute-start.77
  389.5 6.4 collective-permute-start.81
  401.9 6.4 collective-permute-start.85
  414.2 6.4 collective-permute-start.89
  439.5 6.6 collective-permute-start.93
  439.6 6.5 collective-permute-start.94
  452.8 6.6 collective-permute-start.97
  452.9 6.5 collective-permute-start.98
  467.8 6.6 collective-permute-start.101
  467.9 6.5 collective-permute-start.102
  479.7 6.6 collective-permute-start.105
  479.8 6.5 collective-permute-start.106
  491.6 6.8 %collective-permute-start.109 = (f32[8,16,256]{2,1,0:T(8,128)S(1)}, f32[8,16,256]{2,1,0:T(8,128)S(1)}, u32[]{:S(2)}, u32[]{:S(2)}) collective-permute-start(f32[8,16,256]{2,1,0:T(8,128)S(1)} %fusion.171), channel_id=1, source_target_pairs={{0,124},{4,0},{8,4},{12,8},{16,12},{20,16},{24,20},{28,24},{32,28}... | collective-permute-start | bytes 393224 | tf_op jit(solution)/shard_map/ppermute | solution.py:28
  503.4 6.5 collective-permute-start.111
  515.3 7.9 %collective-permute-start.113 = (f32[8,16,256]{2,1,0:T(8,128)S(1)}, f32[8,16,256]{2,1,0:T(8,128)S(1)}, u32[]{:S(2)}, u32[]{:S(2)}) collective-permute-start(f32[8,16,256]{2,1,0:T(8,128)S(1)} %broadcast_select_fusion.6), channel_id=1, source_target_pairs={{0,64},{4,68},{8,72},{12,76},{16,80},{20,84},{24,88},{28,92},{32,9... | collective-permute-start | bytes 393224 | tf_op jit(solution)/shard_map/ppermute | solution.py:28
  593.9 9.2 %collective-permute-start.114 = (f32[1,32,512]{2,1,0:T(8,128)S(1)}, f32[1,32,512]{2,1,0:T(8,128)S(1)}, u32[]{:S(2)}, u32[]{:S(2)}) collective-permute-start(f32[1,32,512]{2,1,0:T(8,128)S(1)} %get-tuple-element.54), channel_id=1, source_target_pairs={{0,4},{4,8},{8,12},{12,16},{16,20},{20,24},{24,28},{28,32},{32,36}... | collective-permute-start | bytes 196616 | tf_op jit(solution)/shard_map/ppermute | solution.py:18
  594.1 9.1 %collective-permute-start.115 = (f32[1,32,512]{2,1,0:T(8,128)S(1)}, f32[1,32,512]{2,1,0:T(8,128)S(1)}, u32[]{:S(2)}, u32[]{:S(2)}) collective-permute-start(f32[1,32,512]{2,1,0:T(8,128)S(1)} %get-tuple-element.55), channel_id=1, source_target_pairs={{4,0},{8,4},{12,8},{16,12},{20,16},{24,20},{28,24},{32,28},{36,32}... | collective-permute-start | bytes 196616 | tf_op jit(solution)/shard_map/ppermute | solution.py:21
  611.3 7.1 %collective-permute-start.118 = (f32[1,32,512]{2,1,0:T(8,128)S(1)}, f32[1,32,512]{2,1,0:T(8,128)S(1)}, u32[]{:S(2)}, u32[]{:S(2)}) collective-permute-start(f32[1,32,512]{2,1,0:T(8,128)S(1)} %get-tuple-element.52), channel_id=1, source_target_pairs={{0,4},{4,8},{8,12},{12,16},{16,20},{20,24},{24,28},{28,32},{32,36}... | collective-permute-start | bytes 196616 | tf_op jit(solution)/shard_map/ppermute | solution.py:18
  611.4 7.0 %collective-permute-start.119 = (f32[1,32,512]{2,1,0:T(8,128)S(1)}, f32[1,32,512]{2,1,0:T(8,128)S(1)}, u32[]{:S(2)}, u32[]{:S(2)}) collective-permute-start(f32[1,32,512]{2,1,0:T(8,128)S(1)} %get-tuple-element.53), channel_id=1, source_target_pairs={{4,0},{8,4},{12,8},{16,12},{20,16},{24,20},{28,24},{32,28},{36,32}... | collective-permute-start | bytes 196616 | tf_op jit(solution)/shard_map/ppermute | solution.py:21
  627.0 7.1 %collective-permute-start.122 = (f32[1,32,512]{2,1,0:T(8,128)S(1)}, f32[1,32,512]{2,1,0:T(8,128)S(1)}, u32[]{:S(2)}, u32[]{:S(2)}) collective-permute-start(f32[1,32,512]{2,1,0:T(8,128)S(1)} %get-tuple-element.50), channel_id=1, source_target_pairs={{0,4},{4,8},{8,12},{12,16},{16,20},{20,24},{24,28},{28,32},{32,36}... | collective-permute-start | bytes 196616 | tf_op jit(solution)/shard_map/ppermute | solution.py:18
  627.1 7.0 %collective-permute-start.123 = (f32[1,32,512]{2,1,0:T(8,128)S(1)}, f32[1,32,512]{2,1,0:T(8,128)S(1)}, u32[]{:S(2)}, u32[]{:S(2)}) collective-permute-start(f32[1,32,512]{2,1,0:T(8,128)S(1)} %get-tuple-element.51), channel_id=1, source_target_pairs={{4,0},{8,4},{12,8},{16,12},{20,16},{24,20},{28,24},{32,28},{36,32}... | collective-permute-start | bytes 196616 | tf_op jit(solution)/shard_map/ppermute | solution.py:21
  642.8 7.1 %collective-permute-start.126 = (f32[1,32,512]{2,1,0:T(8,128)S(1)}, f32[1,32,512]{2,1,0:T(8,128)S(1)}, u32[]{:S(2)}, u32[]{:S(2)}) collective-permute-start(f32[1,32,512]{2,1,0:T(8,128)S(1)} %get-tuple-element.48), channel_id=1, source_target_pairs={{0,4},{4,8},{8,12},{12,16},{16,20},{20,24},{24,28},{28,32},{32,36}... | collective-permute-start | bytes 196616 | tf_op jit(solution)/shard_map/ppermute | solution.py:18
  642.8 7.0 %collective-permute-start.127 = (f32[1,32,512]{2,1,0:T(8,128)S(1)}, f32[1,32,512]{2,1,0:T(8,128)S(1)}, u32[]{:S(2)}, u32[]{:S(2)}) collective-permute-start(f32[1,32,512]{2,1,0:T(8,128)S(1)} %get-tuple-element.49), channel_id=1, source_target_pairs={{4,0},{8,4},{12,8},{16,12},{20,16},{24,20},{28,24},{32,28},{36,32}... | collective-permute-start | bytes 196616 | tf_op jit(solution)/shard_map/ppermute | solution.py:21
  658.0 7.1 %collective-permute-start.130 = (f32[1,32,512]{2,1,0:T(8,128)S(1)}, f32[1,32,512]{2,1,0:T(8,128)S(1)}, u32[]{:S(2)}, u32[]{:S(2)}) collective-permute-start(f32[1,32,512]{2,1,0:T(8,128)S(1)} %get-tuple-element.46), channel_id=1, source_target_pairs={{0,4},{4,8},{8,12},{12,16},{16,20},{20,24},{24,28},{28,32},{32,36}... | collective-permute-start | bytes 196616 | tf_op jit(solution)/shard_map/ppermute | solution.py:18
  658.1 7.0 %collective-permute-start.131 = (f32[1,32,512]{2,1,0:T(8,128)S(1)}, f32[1,32,512]{2,1,0:T(8,128)S(1)}, u32[]{:S(2)}, u32[]{:S(2)}) collective-permute-start(f32[1,32,512]{2,1,0:T(8,128)S(1)} %get-tuple-element.47), channel_id=1, source_target_pairs={{4,0},{8,4},{12,8},{16,12},{20,16},{24,20},{28,24},{32,28},{36,32}... | collective-permute-start | bytes 196616 | tf_op jit(solution)/shard_map/ppermute | solution.py:21
  (114 other events, 1608.4 us)
where the time goes:
time: 685 us; the launch traced here: 674 us
  starting transfers between devices  271 us (40%)
  local copies, waits for them, and re-layouts  164 us (24%)
  waiting for transfers between devices  152 us (22%)
  other arithmetic  83.4 us (12%)
    ppermute x62, starting transfers between devices, with_halo(): lax.ppermute(lax.slice_in_dim(block, 0, width, axis=dim), axis, backward)  222 us
    ppermute x62, waiting for transfers between devices, with_halo(): lax.ppermute(lax.slice_in_dim(block, block.shape[dim] - width, None, axis...  89.6 us
    reshape x2, local copies, waits for them, and re-layouts, restrict(): residue.reshape(extent_x // 2, 2, extent_y // 2, 2, extent_z // 2, 2)  79.6 us
    reshape x2, local copies, waits for them, and re-layouts, prolong(): return spread_out.reshape(2 * extent_x, 2 * extent_y, 2 * extent_z)  54.7 us
    ppermute x10, waiting for transfers between devices, from_behind(): lax.ppermute(x, axis, [(i, (i + by) % devices) for i in range(devices)])  52.7 us
    ppermute x62, starting transfers between devices, with_halo(): lax.ppermute(lax.slice_in_dim(block, block.shape[dim] - width, None, axis...  44 us
    select_n x28, other arithmetic, relaxed(): return jnp.where(chosen, updated, iterate)  34.4 us
    broadcast_in_dim x2, local copies, waits for them, and re-layouts, prolong(): jnp.broadcast_to(coarse[:, None, :, None, :, None], (extent_x, 2, extent_...  25.3 us
  transfers between devices with their start and end apart: 134, of which 92 were waited for; matrix products, arithmetic and copies ran while one was open for 1% of the time, Pallas kernels for 0%

commit v1 on v0

v1 whole, which is shorter than its diff:
```python
import jax
import jax.numpy as jnp
from jax import lax
from jax.experimental import pallas as pl
from jax.experimental.pallas import tpu as pltpu
from jax.sharding import PartitionSpec as P

MESH = pl.DeviceIdType.MESH
F32 = jnp.float32
NW, NN = 32, 4
LOW_SENDS = [(dw, dn) for dw in range(-4, 5) for dn in range(4) if (dw, dn) != (0, 0)]
CORNERS = [(dw, dn) for dw in (-1, 1) for dn in (-1, 1)]
SIDES = [(-1, 0), (1, 0), (0, -1), (0, 1)]


def iota(axis):
    return lax.broadcasted_iota(jnp.int32, (8, 128), axis)


def take(x, index):
    return jnp.take_along_axis(x, index, axis=1, mode="promise_in_bounds")


def split_index(n):
    lane = iota(1)
    width = 128 // n
    block, place = lane // width, lane % width
    return [n * place + (block - a) % n for a in range(n)], block


def split_lanes(parts, index, block):
    n = len(parts)
    gathered = [take(part, index[a]) for a, part in enumerate(parts)]
    out = []
    for t in range(n):
        tile = gathered[(n - 1 - t) % n]
        for place in range(n - 1):
            tile = jnp.where(block == place, gathered[(place - t) % n], tile)
        out.append(tile if t == 0 else pltpu.roll(tile, 128 - t * (128 // n), 1))
    return out


def join_index(n):
    lane = iota(1)
    width = 128 // n
    return [width * ((lane % n + a) % n) + lane // n for a in range(n)], lane // width


def join_lanes(tiles, index, block):
    n = len(tiles)
    turned = [tiles[t] if t == 0 else pltpu.roll(tiles[t], t * (128 // n), 1) for t in range(n)]
    out = []
    for a in range(n):
        tile = turned[(n - 1 - a) % n]
        for place in range(n - 1):
            tile = jnp.where(block == place, turned[(place - a) % n], tile)
        out.append(take(tile, index[a]))
    return out


def down(x):
    return pltpu.roll(x, 1, 0)


def up(x):
    return pltpu.roll(x, 7, 0)


def left(x):
    return pltpu.roll(x, 1, 1)


def right(x):
    return pltpu.roll(x, 127, 1)


class Level:
    def __init__(self, J, T, h, fx, fy, fz, rinv, diag, src, v):
        self.J, self.T = J, T
        self.h, self.fx, self.fy, self.fz = h, fx, fy, fz
        self.rinv, self.diag, self.src, self.v = rinv, diag, src, v

    def cells(self, parity):
        return [(j, t) for j in range(self.J) for t in range(self.T) if (j + t) % 2 == parity]

    def setup(self, b_of, c_of, first, count, plane_lo, plane_hi, row_lo, row_hi):
        J, T = self.J, self.T
        lane = iota(1)
        row = J * iota(0)
        zero = jnp.zeros((8, 128), F32)

        def fill(x, _):
            scale = jnp.where((x >= plane_lo) & (x < plane_hi), 0.5, 0.0).astype(F32)
            for j in range(J):
                inside = (row + j >= row_lo) & (row + j < row_hi)
                for t in range(T):
                    self.h[x, j, t] = jnp.where(inside, b_of(x, j, t) * scale, zero)
            return 0

        lax.fori_loop(first - 1, first + count + 1, fill, 0)

        def open_face(x):
            return jnp.where((x == plane_lo) | (x == plane_hi), 0.0, 1.0).astype(F32)

        for j in range(J):
            for t in range(T):
                self.fx[first, j, t] = (self.h[first - 1, j, t] + self.h[first, j, t]) * open_face(first)

        def build(x, _):
            h = {(j, t): self.h[x, j, t] for j in range(J) for t in range(T)}
            edge_hi = open_face(x + 1)
            for t in range(T):
                real_y = [h[j, t] + (h[j - 1, t] if j else down(h[J - 1, t])) for j in range(J)]
                real_y.append(up(real_y[0]))
                for j in range(J + 1):
                    closed = (row + j == row_lo) | (row + j == row_hi)
                    self.fy[x, j, t] = jnp.where(closed, zero, real_y[j])
                for j in range(J):
                    here = h[j, t]
                    lo_x = self.h[x - 1, j, t] + here
                    hi_x = self.h[x + 1, j, t] + here
                    self.fx[x + 1, j, t] = hi_x * edge_hi
                    if t:
                        lo_z = here + h[j, t - 1]
                        self.fz[x, j, t] = lo_z
                    else:
                        beside = jnp.where(lane == 0, zero, left(h[j, T - 1]))
                        lo_z = here + beside
                        self.fz[x, j, t] = jnp.where(lane == 0, zero, lo_z)
                    if t < T - 1:
                        hi_z = here + h[j, t + 1]
                    else:
                        beside = jnp.where(lane == 127, zero, right(h[j, 0]))
                        hi_z = here + beside
                        self.fz[x, j, T] = jnp.where(lane == 127, zero, hi_z)
                    diag = lo_x + hi_x + real_y[j] + real_y[j + 1] + lo_z + hi_z + c_of(x, j, t)
                    self.diag[x, j, t] = diag
                    self.rinv[x, j, t] = 1.0 / diag
            return 0

        lax.fori_loop(first, first + count, build, 0)

    def pulled(self, x, j, t, get):
        J, T, v = self.J, self.T, self.v
        total = self.fx[x, j, t] * v[x - 1, j, t] + self.fx[x + 1, j, t] * v[x + 1, j, t]
        total += self.fy[x, j, t] * (get(j - 1, t) if j else down(get(J - 1, t)))
        total += self.fy[x, j + 1, t] * (get(j + 1, t) if j < J - 1 else up(get(0, t)))
        total += self.fz[x, j, t] * (get(j, t - 1) if t else left(get(j, T - 1)))
        total += self.fz[x, j, t + 1] * (get(j, t + 1) if t < T - 1 else right(get(j, 0)))
        return total

    def reader(self, x):
        seen = {}

        def get(j, t):
            if (j, t) not in seen:
                seen[j, t] = self.v[x, j, t]
            return seen[j, t]

        return get

    def start(self, first, count):
        def body(i, _):
            for half in (0, 1):
                x = first + 2 * i + half
                for j, t in self.cells((first + half) % 2):
                    self.v[x, j, t] = self.src[x, j, t] * self.rinv[x, j, t]
            return 0

        lax.fori_loop(0, count // 2, body, 0)

    def half_sweep(self, colour, first, count):
        def body(i, _):
            for half in (0, 1):
                x = first + 2 * i + half
                get = self.reader(x)
                for j, t in self.cells((first + half + colour) % 2):
                    total = self.src[x, j, t] + self.pulled(x, j, t, get)
                    self.v[x, j, t] = total * self.rinv[x, j, t]
            return 0

        lax.fori_loop(0, count // 2, body, 0)

    def residual(self, x, j, t, get):
        return self.src[x, j, t] - (self.diag[x, j, t] * get(j, t) - self.pulled(x, j, t, get))

    def restrict_pair(self, x):
        sums = {}
        for half in (0, 1):
            get = self.reader(x + half)
            for j in range(self.J):
                for t in range(self.T):
                    value = self.residual(x + half, j, t, get)
                    key = (j // 2, t // 2)
                    sums[key] = sums[key] + value if key in sums else value
        return {key: 0.5 * value for key, value in sums.items()}


def kernel(rhs, cf, cm, cl, out_v, out_r,
           tb, tc, ts, tv, pk, pk5, py, py5, pc,
           fh, ffx, ffy, ffz, frinv, fdiag, fsrc, fv, stage,
           mt, st, vt, vp, mh, mfx, mfy, mfz, mrinv, mdiag, msrc, mv, mstage, lstage,
           lc, s2own, s2g, lh, lcoef, lsrc, lv, v2t,
           pkv, pkv5, pyv, pyv5, pcv,
           send, recv):
    w = lax.axis_index("wide")
    n = lax.axis_index("narrow")

    def device(dw, dn):
        return (lax.rem(w + (dw + NW), NW), lax.rem(n + (dn + NN), NN))

    barrier = pltpu.get_barrier_semaphore()
    for dw, dn in LOW_SENDS:
        pl.semaphore_signal(barrier, inc=1, device_id=device(dw, dn), device_id_type=MESH)

    count = [0]

    def remote(src, dst, dw, dn):
        k = count[0]
        count[0] += 1
        copy = pltpu.make_async_remote_copy(
            src_ref=src, dst_ref=dst, send_sem=send.at[k], recv_sem=recv.at[k],
            device_id=device(dw, dn), device_id_type=MESH)
        copy.start()
        return copy

    def landed(copies):
        for copy in copies:
            copy.wait_recv()

    everything = []

    index4, block4 = split_index(4)

    def to_split(read, target):
        def body(x, _):
            for r in range(4):
                parts = [read(x, r, a) for a in range(4)]
                for t, tile in enumerate(split_lanes(parts, index4, block4)):
                    target[6 + x, t, 8 + 8 * r:16 + 8 * r, :] = tile
            return 0

        lax.fori_loop(0, 16, body, 0)

    to_split(lambda x, r, a: cf[0, x, 8 * r:8 * r + 8, 128 * a:128 * a + 128], tb)
    to_split(lambda x, r, a: cf[1, x, 8 * r:8 * r + 8, 128 * a:128 * a + 128], tc)
    to_split(lambda x, r, a: rhs[x, 8 * r:8 * r + 8, 128 * a:128 * a + 128], ts)

    def pack(field, packed, which):
        def body(p, _):
            for t in range(4):
                for half in (0, 1):
                    x = 6 + 2 * p + half
                    packed[0, which, p, t, 4 * half:4 * half + 4, :] = field[x, t, 8:12, :]
                    packed[1, which, p, t, 4 * half:4 * half + 4, :] = field[x, t, 36:40, :]
            return 0

        lax.fori_loop(0, 8, body, 0)

    def pack_fifth(field, packed):
        for x in range(16):
            for t in range(4):
                packed[0, t, x:x + 1, :] = field[6 + x, t, 12:13, :]
                packed[1, t, x:x + 1, :] = field[6 + x, t, 35:36, :]

    def send_planes(field, layers):
        own = pl.ds(8, 32)
        return [
            remote(field.at[pl.ds(6, layers), :, own], field.at[pl.ds(22, layers), :, own], -1, 0),
            remote(field.at[pl.ds(22 - layers, layers), :, own], field.at[pl.ds(6 - layers, layers), :, own], 1, 0),
        ]

    def send_rows(packed, packed5, got, got5, got_corner):
        copies = [
            remote(packed.at[0], got.at[1], 0, -1),
            remote(packed.at[1], got.at[0], 0, 1),
            remote(packed5.at[0], got5.at[1], 0, -1),
            remote(packed5.at[1], got5.at[0], 0, 1),
        ]
        for dw, dn in CORNERS:
            side, pairs = (dn + 1) // 2, pl.ds(0 if dw < 0 else 6, 2)
            there_w, there_n = (1 - dw) // 2, (1 - dn) // 2
            copies.append(remote(packed.at[side, :, pairs], got_corner.at[2 * there_w + there_n], dw, dn))
        return copies

    def unpack(field, got, got_corner, which):
        def place(x, t, half, lower, upper):
            field[x, t, 4:8, :] = lower[4 * half:4 * half + 4]
            field[x, t, 40:44, :] = upper[4 * half:4 * half + 4]

        def body(p, _):
            for t in range(4):
                lower, upper = got[0, which, p, t], got[1, which, p, t]
                for half in (0, 1):
                    place(6 + 2 * p + half, t, half, lower, upper)
            return 0

        lax.fori_loop(0, 8, body, 0)
        for there_w in (0, 1):
            for p in range(2):
                for t in range(4):
                    lower = got_corner[2 * there_w, which, p, t]
                    upper = got_corner[2 * there_w + 1, which, p, t]
                    for half in (0, 1):
                        place((22 if there_w else 2) + 2 * p + half, t, half, lower, upper)

    def unpack_fifth(field, got5):
        for x in range(16):
            for t in range(4):
                field[6 + x, t, 3:4, :] = got5[0, t, x:x + 1, :]
                field[6 + x, t, 44:45, :] = got5[1, t, x:x + 1, :]

    pack(ts, pk, 0)
    pack(tc, pk, 1)
    pack(tb, pk, 2)
    pack_fifth(tb, pk5)

    pl.semaphore_wait(barrier, len(LOW_SENDS))

    round0 = send_planes(tb, 5) + send_planes(tc, 4) + send_planes(ts, 4)
    round0 += send_rows(pk, pk5, py, py5, pc)
    everything += round0

    index2, block2 = split_index(2)

    def split_mid(x, _):
        for which in (0, 1):
            for r in range(2):
                parts = [cm[which, x, 8 * r:8 * r + 8, 128 * a:128 * a + 128] for a in range(2)]
                for t, tile in enumerate(split_lanes(parts, index2, block2)):
                    mt[which, 8 + x, t, 8 + 8 * r:16 + 8 * r, :] = tile
        return 0

    lax.fori_loop(0, 8, split_mid, 0)

    def mid_slices(dw, dn):
        planes = pl.ds(8, 8)
        planes_there = pl.ds(8 - 8 * dw, 8)
        rows = pl.ds(8, 16) if dn == 0 else pl.ds(8 if dn < 0 else 16, 8)
        rows_there = pl.ds(8, 16) if dn == 0 else pl.ds(24 if dn < 0 else 0, 8)
        return planes, rows, planes_there, rows_there

    def send_mid(field, pair):
        copies = []
        for dw, dn in SIDES + CORNERS:
            planes, rows, planes_there, rows_there = mid_slices(dw, dn)
            if pair:
                src = field.at[:, planes, :, rows]
                dst = field.at[:, planes_there, :, rows_there]
            else:
                src = field.at[planes, :, rows]
                dst = field.at[planes_there, :, rows_there]
            copies.append(remote(src, dst, dw, dn))
        return copies

    mid_coef_copies = send_mid(mt, True)
    everything += mid_coef_copies

    def send_low(src, dst_of):
        return [remote(src, dst_of(4 - dw), dw, dn) for dw, dn in LOW_SENDS]

    low_coef_copies = send_low(cl, lambda slot: lc.at[:, pl.ds(4 * slot, 4), n])
    everything += low_coef_copies
    for which in (0, 1):
        for x in range(4):
            lc[which, 16 + x, n] = cl[which, x]

    landed(round0)
    for which, field in enumerate((ts, tc, tb)):
        unpack(field, py, pc, which)
    unpack_fifth(tb, py5)

    row_lo = lambda rows: jnp.where(n == 0, rows, 0)
    row_hi = lambda edge, last: jnp.where(n == NN - 1, edge, last)
    first_box, last_box = w == 0, w == NW - 1

    fine = Level(6, 4, fh, ffx, ffy, ffz, frinv, fdiag, fsrc, fv)
    fine.setup(
        lambda x, j, t: tb[x, t, pl.ds(j, 8, stride=6), :],
        lambda x, j, t: tc[x, t, pl.ds(j, 8, stride=6), :],
        2, 24,
        jnp.where(first_box, 6, -1), jnp.where(last_box, 22, 99),
        row_lo(8), row_hi(40, 48))

    def load_fine(x, _):
        for j in range(6):
            for t in range(4):
                fsrc[x, j, t] = ts[x, t, pl.ds(j, 8, stride=6), :]
        return 0

    lax.fori_loop(2, 26, load_fine, 0)
    fine.start(2, 24)
    fine.half_sweep(1, 3, 22)
    fine.half_sweep(0, 4, 20)
    fine.half_sweep(1, 5, 18)

    def restrict_fine(i, _):
        for (j, t), value in fine.restrict_pair(6 + 2 * i).items():
            mstage[i, t, pl.ds(4 + j, 8, stride=3), :] = value
        for t in range(2):
            st[8 + i, t, 8:24, :] = mstage[i, t, 8:24, :]
        return 0

    lax.fori_loop(0, 8, restrict_fine, 0)

    round1 = send_mid(st, False)
    everything += round1

    def store_fine(x, _):
        for j in range(6):
            for t in range(4):
                tv[x, t, pl.ds(j, 8, stride=6), :] = fv[x, j, t]
        return 0

    lax.fori_loop(6, 22, store_fine, 0)
    pack(tv, pkv, 0)
    pack_fifth(tv, pkv5)
    fine_copies = send_planes(tv, 5) + send_rows(pkv, pkv5, pyv, pyv5, pcv)
    everything += fine_copies

    landed(mid_coef_copies)
    mid = Level(4, 2, mh, mfx, mfy, mfz, mrinv, mdiag, msrc, mv)
    mid.setup(
        lambda x, j, t: mt[0, x, t, pl.ds(j, 8, stride=4), :],
        lambda x, j, t: mt[1, x, t, pl.ds(j, 8, stride=4), :],
        1, 22,
        jnp.where(first_box, 8, -1), jnp.where(last_box, 16, 99),
        row_lo(8), row_hi(24, 32))

    landed(round1)

    def load_mid(x, _):
        for j in range(4):
            for t in range(2):
                msrc[x, j, t] = st[x, t, pl.ds(j, 8, stride=4), :]
        return 0

    lax.fori_loop(2, 22, load_mid, 0)
    mid.start(4, 16)
    mid.half_sweep(1, 5, 14)
    mid.half_sweep(0, 6, 12)
    mid.half_sweep(1, 7, 10)

    def restrict_mid(i, _):
        for (j, t), value in mid.restrict_pair(8 + 2 * i).items():
            lstage[i, pl.ds(j, 8, stride=2), :] = value
        value = lstage[i, 4:12, :]
        s2own[i] = value
        s2g[16 + i, n] = value
        return 0

    lax.fori_loop(0, 4, restrict_mid, 0)

    round2 = send_low(s2own, lambda slot: s2g.at[pl.ds(4 * slot, 4), n])
    everything += round2

    def store_mid(x, _):
        for j in range(4):
            for t in range(2):
                mstage[x, t, pl.ds(j, 8, stride=4), :] = mv[8 + x, j, t]
        for t in range(2):
            vt[8 + x, t, 8:24, :] = mstage[x, t, 8:24, :]
        return 0

    lax.fori_loop(0, 8, store_mid, 0)
    mid_copies = send_mid(vt, False)
    everything += mid_copies

    landed(low_coef_copies)
    lane, sub = iota(1), iota(0)
    par = (lane + sub) % 2 == 0
    zero = jnp.zeros((8, 128), F32)
    low_lo = 16 - 4 * w
    low_hi = 16 + 4 * (NW - w)

    for r in range(4):
        lh[0, r] = zero
        lh[37, r] = zero

    def fill_low(i, _):
        scale = jnp.where((i >= low_lo) & (i < low_hi), 0.5, 0.0).astype(F32)
        for r in range(4):
            lh[1 + i, r] = lc[0, i, r] * scale
        return 0

    lax.fori_loop(0, 36, fill_low, 0)

    def open_low(i):
        return jnp.where((i == low_lo) | (i == low_hi), 0.0, 1.0).astype(F32)

    def build_low(p, _):
        i = 2 * p
        edge_lo, edge_hi = open_low(i), open_low(i + 2)
        h = [[lh[i + k, r] for r in range(4)] for k in range(4)]
        for r in range(4):
            lo_x = h[0][r] + h[1][r]
            in_x = h[1][r] + h[2][r]
            hi_x = h[2][r] + h[3][r]
            faces, diags = [], []
            for k in (1, 2):
                here = h[k][r]
                below = jnp.where(sub == 0, down(h[k][r - 1]) if r else zero, down(here))
                above = jnp.where(sub == 7, up(h[k][r + 1]) if r < 3 else zero, up(here))
                lo_y, hi_y = here + below, here + above
                lo_z = here + jnp.where(lane == 0, zero, left(here))
                hi_z = here + jnp.where(lane == 127, zero, right(here))
                out_x = lo_x if k == 1 else hi_x
                diags.append(in_x + out_x + lo_y + hi_y + lo_z + hi_z + lc[1, i + k - 1, r])
                if r == 0:
                    lo_y = jnp.where(sub == 0, zero, lo_y)
                if r == 3:
                    hi_y = jnp.where(sub == 7, zero, hi_y)
                faces.append((out_x * (edge_lo if k == 1 else edge_hi), lo_y, hi_y,
                              jnp.where(lane == 0, zero, lo_z), jnp.where(lane == 127, zero, hi_z)))
            for colour in (0, 1):
                lcoef[p, r, colour, 0] = in_x
                for k in range(5):
                    a, b = faces[colour][k], faces[1 - colour][k]
                    lcoef[p, r, colour, 1 + k] = jnp.where(par, a, b)
                lcoef[p, r, colour, 6] = 1.0 / jnp.where(par, diags[colour], diags[1 - colour])
        return 0

    lax.fori_loop(0, 18, build_low, 0)

    landed(round2)

    def load_low(p, _):
        for r in range(4):
            a, b = s2g[2 * p, r], s2g[2 * p + 1, r]
            lsrc[0, p, r] = jnp.where(par, a, b)
            lsrc[1, p, r] = jnp.where(par, b, a)
            lv[0, p, r] = lsrc[0, p, r] * lcoef[p, r, 0, 6]
        return 0

    lax.fori_loop(0, 18, load_low, 0)

    def low_half_sweep(colour, first, last):
        def body(p, _):
            other = [lv[1 - colour, p, r] for r in range(4)]
            downs = [down(value) for value in other]
            ups = [up(value) for value in other]
            for r in range(4):
                coef = lambda k: lcoef[p, r, colour, k]
                before, after = lv[1 - colour, p - 1, r], lv[1 - colour, p + 1, r]
                out = jnp.where(par, before, after) if colour == 0 else jnp.where(par, after, before)
                total = lsrc[colour, p, r] + coef(0) * other[r] + coef(1) * out
                total += coef(2) * jnp.where(sub == 0, downs[r - 1], downs[r])
                total += coef(3) * jnp.where(sub == 7, ups[(r + 1) % 4], ups[r])
                total += coef(4) * left(other[r]) + coef(5) * right(other[r])
                lv[colour, p, r] = total * coef(6)
            return 0

        lax.fori_loop(first, last + 1, body, 0)

    for k in range(2, 13):
        low_half_sweep((k + 1) % 2, k // 2, 17 - k // 2)

    for i in range(12):
        v2t[i, 0:8, :] = zero
        v2t[i, 40:48, :] = zero
    for p in range(6):
        for r in range(4):
            a, b = lv[0, 6 + p, r], lv[1, 6 + p, r]
            v2t[2 * p, 8 + 8 * r:16 + 8 * r, :] = jnp.where(par, a, b)
            v2t[2 * p + 1, 8 + 8 * r:16 + 8 * r, :] = jnp.where(par, b, a)

    landed(mid_copies)

    def correct_mid(i, _):
        for j in range(4):
            coarse = v2t[i, pl.ds(8 * n + 4 + j // 2, 8, stride=2), :]
            for half in (0, 1):
                for t in range(2):
                    x = 2 * i + half
                    mv[x, j, t] = vt[x, t, pl.ds(j, 8, stride=4), :] + coarse
        return 0

    lax.fori_loop(0, 12, correct_mid, 0)
    mid.half_sweep(0, 2, 20)
    mid.half_sweep(1, 3, 18)
    mid.half_sweep(0, 4, 16)
    mid.half_sweep(1, 5, 14)

    def spread_mid(x, _):
        for j in range(4):
            for t in range(2):
                vp[x, t, pl.ds(j, 8, stride=4), :] = mv[x, j, t]
        return 0

    lax.fori_loop(5, 19, spread_mid, 0)

    landed(fine_copies)
    unpack(tv, pyv, pcv, 0)
    unpack_fifth(tv, pyv5)

    def correct_fine(q, _):
        for j in range(3):
            for t in range(2):
                coarse = vp[q + 5, t, pl.ds(4 + j, 8, stride=3), :]
                for half in (0, 1):
                    x = 2 * q + half
                    for jj in (2 * j, 2 * j + 1):
                        for tt in (2 * t, 2 * t + 1):
                            if (half + jj + tt) % 2 == 1:
                                fv[x, jj, tt] = tv[x, tt, pl.ds(jj, 8, stride=6), :] + coarse
        return 0

    lax.fori_loop(0, 14, correct_fine, 0)
    fine.half_sweep(0, 2, 24)
    fine.half_sweep(1, 3, 22)
    fine.half_sweep(0, 4, 20)
    fine.half_sweep(1, 5, 18)

    join4, join_block4 = join_index(4)

    def finish(x, _):
        get = fine.reader(6 + x)
        for j in range(6):
            for t in range(4):
                stage[0, t, pl.ds(j, 8, stride=6), :] = get(j, t)
                stage[1, t, pl.ds(j, 8, stride=6), :] = fine.residual(6 + x, j, t, get)
        for k, out in enumerate((out_v, out_r)):
            for r in range(4):
                tiles = [stage[k, t, 8 + 8 * r:16 + 8 * r, :] for t in range(4)]
                for a, part in enumerate(join_lanes(tiles, join4, join_block4)):
                    out[x, 8 * r:8 * r + 8, 128 * a:128 * a + 128] = part
        return 0

    lax.fori_loop(0, 16, finish, 0)
    for copy in everything:
        copy.wait_send()


N_COPIES = 14 + 8 + 35 + 8 + 10 + 35 + 8


def vmem(*shape):
    return pltpu.VMEM(shape, F32)


def v_cycle(rhs, cf, cm, cl):
    vm = pl.BlockSpec(memory_space=pltpu.VMEM)
    shape = jax.ShapeDtypeStruct(rhs.shape, F32)
    fine_t = (28, 4, 48, 128)
    fine_a = (28, 6, 4, 8, 128)
    mid_t = (24, 2, 32, 128)
    mid_a = (24, 4, 2, 8, 128)
    scratch = [
        vmem(*fine_t), vmem(*fine_t), vmem(*fine_t), vmem(*fine_t),
        vmem(2, 3, 8, 4, 8, 128), vmem(2, 4, 16, 128),
        vmem(2, 3, 8, 4, 8, 128), vmem(2, 4, 16, 128), vmem(4, 3, 2, 4, 8, 128),
        vmem(*fine_a), vmem(*fine_a), vmem(28, 7, 4, 8, 128), vmem(28, 6, 5, 8, 128),
        vmem(*fine_a), vmem(*fine_a), vmem(*fine_a), vmem(*fine_a), vmem(2, 4, 48, 128),
        vmem(2, *mid_t), vmem(*mid_t), vmem(*mid_t), vmem(*mid_t),
        vmem(*mid_a), vmem(*mid_a), vmem(24, 5, 2, 8, 128), vmem(24, 4, 3, 8, 128),
        vmem(*mid_a), vmem(*mid_a), vmem(*mid_a), vmem(*mid_a),
        vmem(8, 2, 32, 128), vmem(4, 16, 128),
        vmem(2, 36, 4, 8, 128), vmem(4, 8, 128), vmem(36, 4, 8, 128), vmem(38, 4, 8, 128),
        vmem(18, 4, 2, 7, 8, 128), vmem(2, 18, 4, 8, 128), vmem(2, 18, 4, 8, 128), vmem(12, 48, 128),
        vmem(2, 1, 8, 4, 8, 128), vmem(2, 4, 16, 128),
        vmem(2, 1, 8, 4, 8, 128), vmem(2, 4, 16, 128), vmem(4, 1, 2, 4, 8, 128),
        pltpu.SemaphoreType.DMA((N_COPIES,)), pltpu.SemaphoreType.DMA((N_COPIES,)),
    ]
    return pl.pallas_call(
        kernel,
        out_shape=(shape, shape),
        in_specs=[vm] * 4,
        out_specs=(vm, vm),
        scratch_shapes=scratch,
        compiler_params=pltpu.CompilerParams(
            collective_id=0, has_side_effects=True, vmem_limit_bytes=60 * 2**20),
    )(rhs, cf, cm, cl)


def on_device(rhs, cf, cm, cl, offset):
    def moved(k):
        pairs = [((i + k) % NW, i) for i in range(NW)]
        return lambda a, b: (lax.ppermute(a, "wide", pairs), lax.ppermute(b, "wide", pairs))

    cm, cl = lax.switch(offset[0] - 1, [moved(k) for k in range(1, NW)], cm, cl)
    return v_cycle(rhs, cf, cm, cl)


def solution(mesh):
    return jax.shard_map(
        on_device,
        mesh=mesh,
        in_specs=(
            P("wide", "narrow", None),
            P(None, "wide", "narrow", None),
            P(None, "wide", "narrow", None),
            P(None, "wide", "narrow", None),
            P(),
        ),
        out_specs=(P("wide", "narrow", None), P("wide", "narrow", None)),
        check_vma=False,
    )
```

time: 685 us -> 134 us (0.20)
  the two profiles are of different devices: /device:TPU:0 before, /device:TPU:1 now
where the time goes in v1:
time: 134 us; the launch traced here: 133 us
  Pallas kernels  103 us (77%)
  starting transfers between devices  19.6 us (15%)
  waiting for transfers between devices  5.96 us (4%)
  local copies, waits for them, and re-layouts  3.35 us (2%)
    pallas_call x1, Pallas kernels, v_cycle(): pl.pallas_call(kernel, out_shape=(shape, shape), in_specs=[vm] * 4, out_s...  103 us
    ppermute x1, starting transfers between devices, moved(): lax.ppermute(a, 'wide', pairs)  10.7 us
    ppermute x1, starting transfers between devices, moved(): lax.ppermute(b, 'wide', pairs)  8.9 us
    ppermute x1, waiting for transfers between devices, moved(): lax.ppermute(b, 'wide', pairs)  5.95 us
    unnamed x4, local copies, waits for them, and re-layouts  3.35 us
  transfers between devices with their start and end apart: 2, of which 1 were waited for; matrix products, arithmetic and copies ran while one was open for 0% of the time, Pallas kernels for 0%

profile of v1, /device:TPU:1, one launch (start us, length us, event | category | flops | bytes accessed | tf_op | source)
XLA Modules:
  0.0 133.1 jit_solution(13305103297584278419)
XLA Ops:
  1.3 25.6 %conditional.1 = (f32[2,8,16,256]{3,2,1,0:T(8,128)}, f32[2,4,8,128]{3,2,1,0:T(8,128)}) conditional(s32[]{:T(128)} %bitcast, (f32[2,8,16,256]{3,2,1,0:T(8,128)}, f32[2,4,8,128]{3,2,1,0:T(8,128)}) %tuple.131, (f32[2,8,16,256]{3,2,1,0:T(8,128)}, f32[2,4,8,128]{3,2,1,0:T(8,128)}) %tuple.131, ...), branch_computations={%region_0.0_spmd, %region_1.0_spmd, %region_2.0_spmd, %region_3.0_... | conditional | bytes 1179744 | solution.py:680
  1.3 10.7 %collective-permute-start.20 = (f32[2,8,16,256]{3,2,1,0:T(8,128)}, f32[2,8,16,256]{3,2,1,0:T(8,128)}, u32[]{:S(2)}, u32[]{:S(2)}) collective-permute-start(f32[2,8,16,256]{3,2,1,0:T(8,128)} %get-tuple-element.144), channel_id=1, source_target_pairs={{44,0},{48,4},{52,8},{56,12},{60,16},{64,20},{68,24},{72,28},{76,3... | collective-permute-start | bytes 786440 | tf_op jit(solution)/shard_map/cond/branch_10_fun/ppermute | solution.py:678
  12.0 8.9 %collective-permute-start.21 = (f32[2,4,8,128]{3,2,1,0:T(8,128)}, f32[2,4,8,128]{3,2,1,0:T(8,128)}, u32[]{:S(2)}, u32[]{:S(2)}) collective-permute-start(f32[2,4,8,128]{3,2,1,0:T(8,128)} %get-tuple-element.145), channel_id=1, source_target_pairs={{44,0},{48,4},{52,8},{56,12},{60,16},{64,20},{68,24},{72,28},{76,3... | collective-permute-start | bytes 98312 | tf_op jit(solution)/shard_map/cond/branch_10_fun/ppermute | solution.py:678
  20.9 6.0 %collective-permute-done.21 = f32[2,4,8,128]{3,2,1,0:T(8,128)} collective-permute-done((f32[2,4,8,128]{3,2,1,0:T(8,128)}, f32[2,4,8,128]{3,2,1,0:T(8,128)}, u32[]{:S(2)}, u32[]{:S(2)}) %collective-permute-start.21) | collective-permute-done | bytes 32800 | tf_op jit(solution)/shard_map/cond/branch_10_fun/ppermute | solution.py:678
  26.9 0.0 collective-permute-done.20
  26.9 102.9 %shard_map.68 = (f32[16,32,512]{2,1,0:T(8,128)}, f32[16,32,512]{2,1,0:T(8,128)}) custom-call(f32[16,32,512]{2,1,0:T(8,128)} %rhs.1, f32[2,16,32,512]{3,2,1,0:T(8,128)} %cf.1, f32[2,8,16,256]{3,2,1,0:T(8,128)} %get-tuple-element.190.cm, f32[2,4,8,128]{3,2,1,0:T(8,128)} %get-tuple-element.191.cl), custom_call_target="tpu_custom_call" | custom-call | tf_op jit(solution)/shard_map/pallas_call | solution.py:664
  129.7 0.0 copy-start
  129.7 2.4 %copy.72 = f32[16,32,512]{2,1,0:T(8,128)} copy(f32[16,32,512]{2,1,0:T(8,128)} %get-tuple-element.256) | data formatting | bytes 2097152
  132.1 0.0 copy-done
  132.1 1.0 copy.73
Async XLA Ops:
  1.3 25.6 %collective-permute-start.20 = (f32[2,8,16,256]{3,2,1,0:T(8,128)}, f32[2,8,16,256]{3,2,1,0:T(8,128)}, u32[]{:S(2)}, u32[]{:S(2)}) collective-permute-start(f32[2,8,16,256]{3,2,1,0:T(8,128)} %get-tuple-element.144), channel_id=1, source_target_pairs={{44,0},{48,4},{52,8},{56,12},{60,16},{64,20},{68,24},{72,28},{76,3... | collective-permute-start | bytes 786440 | tf_op jit(solution)/shard_map/cond/branch_10_fun/ppermute | solution.py:678
  12.0 14.8 %collective-permute-start.21 = (f32[2,4,8,128]{3,2,1,0:T(8,128)}, f32[2,4,8,128]{3,2,1,0:T(8,128)}, u32[]{:S(2)}, u32[]{:S(2)}) collective-permute-start(f32[2,4,8,128]{3,2,1,0:T(8,128)} %get-tuple-element.145), channel_id=1, source_target_pairs={{44,0},{48,4},{52,8},{56,12},{60,16},{64,20},{68,24},{72,28},{76,3... | collective-permute-start | bytes 98312 | tf_op jit(solution)/shard_map/cond/branch_10_fun/ppermute | solution.py:678
  129.7 2.4 %copy-start = (f32[16,32,512]{2,1,0:T(8,128)S(1)}, f32[16,32,512]{2,1,0:T(8,128)}, u32[]{:S(2)}) copy-start(f32[16,32,512]{2,1,0:T(8,128)} %get-tuple-element.257) | copy-start | bytes 3145732

commit v2 on v1

--- a/solution.py
+++ b/solution.py
@@ -8,9 +8,15 @@
 MESH = pl.DeviceIdType.MESH
 F32 = jnp.float32
 NW, NN = 32, 4
-LOW_SENDS = [(dw, dn) for dw in range(-4, 5) for dn in range(4) if (dw, dn) != (0, 0)]
+LOW_SENDS = [(dw, dn) for dw in (-4, 4, -2, 2, 0) for dn in (-1, 0, 1, 2)
+             if (dw, dn) not in ((0, 0), (-4, 2), (4, 2))]
 CORNERS = [(dw, dn) for dw in (-1, 1) for dn in (-1, 1)]
 SIDES = [(-1, 0), (1, 0), (0, -1), (0, 1)]
+GREETED = SIDES + CORNERS + [(-2, 0), (2, 0), (-4, 0), (4, 0)]
+NEAR = [(dx, dy) for dx in range(1, 5) for dy in range(1, 5)]
+CORNER_BC = [(f, dx, dy) for f in (0, 1) for dx, dy in NEAR if dx + dy <= 5 - f]
+CORNER_S = [(0, dx, dy) for dx, dy in NEAR if dx + dy <= 4]
+CORNER_V = [(0, dx, dy) for dx, dy in NEAR if dx + dy <= 5]
 
 
 def iota(axis):
@@ -79,6 +85,9 @@
         self.J, self.T = J, T
         self.h, self.fx, self.fy, self.fz = h, fx, fy, fz
         self.rinv, self.diag, self.src, self.v = rinv, diag, src, v
+
+    def unroll(self, steps):
+        return 1 if self.T == 4 else 2 if steps % 2 == 0 else 3 if steps % 3 == 0 else 1
 
     def cells(self, parity):
         return [(j, t) for j in range(self.J) for t in range(self.T) if (j + t) % 2 == parity]
@@ -138,23 +147,23 @@
                     self.rinv[x, j, t] = 1.0 / diag
             return 0
 
-        lax.fori_loop(first, first + count, build, 0)
-
-    def pulled(self, x, j, t, get):
-        J, T, v = self.J, self.T, self.v
-        total = self.fx[x, j, t] * v[x - 1, j, t] + self.fx[x + 1, j, t] * v[x + 1, j, t]
+        lax.fori_loop(first, first + count, build, 0, unroll=self.unroll(count))
+
+    def pulled(self, x, j, t, colour, get):
+        J, T, other = self.J, self.T, self.v[1 - colour]
+        total = self.fx[x, j, t] * other[x - 1, j, t // 2] + self.fx[x + 1, j, t] * other[x + 1, j, t // 2]
         total += self.fy[x, j, t] * (get(j - 1, t) if j else down(get(J - 1, t)))
         total += self.fy[x, j + 1, t] * (get(j + 1, t) if j < J - 1 else up(get(0, t)))
         total += self.fz[x, j, t] * (get(j, t - 1) if t else left(get(j, T - 1)))
         total += self.fz[x, j, t + 1] * (get(j, t + 1) if t < T - 1 else right(get(j, 0)))
         return total
 
-    def reader(self, x):
+    def reader(self, x, parity):
         seen = {}
 
         def get(j, t):
             if (j, t) not in seen:
-                seen[j, t] = self.v[x, j, t]
+                seen[j, t] = self.v[(parity + j + t) % 2][x, j, t // 2]
             return seen[j, t]
 
         return get
@@ -164,53 +173,69 @@
             for half in (0, 1):
                 x = first + 2 * i + half
                 for j, t in self.cells((first + half) % 2):
-                    self.v[x, j, t] = self.src[x, j, t] * self.rinv[x, j, t]
+                    self.v[0][x, j, t // 2] = self.src[x, j, t] * self.rinv[x, j, t]
             return 0
 
-        lax.fori_loop(0, count // 2, body, 0)
+        lax.fori_loop(0, count // 2, body, 0, unroll=self.unroll(count // 2))
 
     def half_sweep(self, colour, first, count):
         def body(i, _):
             for half in (0, 1):
                 x = first + 2 * i + half
-                get = self.reader(x)
+                get = self.reader(x, (first + half) % 2)
                 for j, t in self.cells((first + half + colour) % 2):
-                    total = self.src[x, j, t] + self.pulled(x, j, t, get)
-                    self.v[x, j, t] = total * self.rinv[x, j, t]
+                    total = self.src[x, j, t] + self.pulled(x, j, t, colour, get)
+                    self.v[colour][x, j, t // 2] = total * self.rinv[x, j, t]
             return 0
 
-        lax.fori_loop(0, count // 2, body, 0)
-
-    def residual(self, x, j, t, get):
-        return self.src[x, j, t] - (self.diag[x, j, t] * get(j, t) - self.pulled(x, j, t, get))
+        lax.fori_loop(0, count // 2, body, 0, unroll=self.unroll(count // 2))
+
+    def residual(self, x, parity, j, t, get):
+        pulled = self.pulled(x, j, t, (parity + j + t) % 2, get)
+        return self.src[x, j, t] - (self.diag[x, j, t] * get(j, t) - pulled)
 
     def restrict_pair(self, x):
         sums = {}
         for half in (0, 1):
-            get = self.reader(x + half)
+            get = self.reader(x + half, half)
             for j in range(self.J):
                 for t in range(self.T):
-                    value = self.residual(x + half, j, t, get)
+                    value = self.residual(x + half, half, j, t, get)
                     key = (j // 2, t // 2)
                     sums[key] = sums[key] + value if key in sums else value
         return {key: 0.5 * value for key, value in sums.items()}
 
 
-def kernel(rhs, cf, cm, cl, out_v, out_r,
-           tb, tc, ts, tv, pk, pk5, py, py5, pc,
-           fh, ffx, ffy, ffz, frinv, fdiag, fsrc, fv, stage,
-           mt, st, vt, vp, mh, mfx, mfy, mfz, mrinv, mdiag, msrc, mv, mstage, lstage,
-           lc, s2own, s2g, lh, lcoef, lsrc, lv, v2t,
-           pkv, pkv5, pyv, pyv5, pcv,
+def kernel(rhs_hbm, cf_hbm, cm_hbm, cl_hbm, hbm_v, hbm_r,
+           rhs, cf, cm, cl, in_sem, out_sem,
+           tb, tc, ts, tv, pk, pk5, pkc, pkcs, py, py5, pc, pcs,
+           fh, ffx, ffy, ffz, frinv, fdiag, fsrc, fv0, fv1,
+           mt, st, vt, vp, mh, mfx, mfy, mfz, mrinv, mdiag, msrc, mv0, mv1, mstage, lstage,
+           lc, s2own, s2g, lh, lcoef, lsrc, lv0, lv1, v2t,
+           pkv, pkv5, pkvc, pyv, pyv5, pcv,
            send, recv):
     w = lax.axis_index("wide")
     n = lax.axis_index("narrow")
+    core = lax.rem(w, 2)
 
     def device(dw, dn):
         return (lax.rem(w + (dw + NW), NW), lax.rem(n + (dn + NN), NN))
 
+    loads = [pltpu.make_async_copy(cf_hbm.at[0], cf.at[0], in_sem.at[0]),
+             pltpu.make_async_copy(cf_hbm.at[1], cf.at[1], in_sem.at[1]),
+             pltpu.make_async_copy(rhs_hbm, rhs, in_sem.at[2]),
+             pltpu.make_async_copy(cm_hbm, cm, in_sem.at[3]),
+             pltpu.make_async_copy(cl_hbm, cl, in_sem.at[4])]
+    for load in loads:
+        load.start()
+    ones, zeros = jnp.ones((8, 128), F32), jnp.zeros((8, 128), F32)
+    for x in (*range(8), *range(32, 40)):
+        for r in range(4):
+            lc[0, x, r] = ones
+            lc[1, x, r] = ones
+            s2g[x, r] = zeros
     barrier = pltpu.get_barrier_semaphore()
-    for dw, dn in LOW_SENDS:
+    for dw, dn in GREETED:
         pl.semaphore_signal(barrier, inc=1, device_id=device(dw, dn), device_id_type=MESH)
 
     count = [0]
@@ -242,10 +267,6 @@
 
         lax.fori_loop(0, 16, body, 0)
 
-    to_split(lambda x, r, a: cf[0, x, 8 * r:8 * r + 8, 128 * a:128 * a + 128], tb)
-    to_split(lambda x, r, a: cf[1, x, 8 * r:8 * r + 8, 128 * a:128 * a + 128], tc)
-    to_split(lambda x, r, a: rhs[x, 8 * r:8 * r + 8, 128 * a:128 * a + 128], ts)
-
     def pack(field, packed, which):
         def body(p, _):
             for t in range(4):
@@ -270,20 +291,35 @@
             remote(field.at[pl.ds(22 - layers, layers), :, own], field.at[pl.ds(6 - layers, layers), :, own], 1, 0),
         ]
 
-    def send_rows(packed, packed5, got, got5, got_corner):
-        copies = [
-            remote(packed.at[0], got.at[1], 0, -1),
-            remote(packed.at[1], got.at[0], 0, 1),
-            remote(packed5.at[0], got5.at[1], 0, -1),
-            remote(packed5.at[1], got5.at[0], 0, 1),
-        ]
+    def pack_corners(fields, rows, packed):
+        for cw in (0, 1):
+            for cn in (0, 1):
+                for r, (f, dx, dy) in enumerate(rows):
+                    x = 22 - dx if cw else 5 + dx
+                    y = 40 - dy if cn else 7 + dy
+                    for t in range(4):
+                        packed[2 * cw + cn, t, r:r + 1, :] = fields[f][x, t, y:y + 1, :]
+
+    def unpack_corners(fields, rows, got):
+        for cw in (0, 1):
+            for cn in (0, 1):
+                for r, (f, dx, dy) in enumerate(rows):
+                    x = 21 + dx if cw else 6 - dx
+                    y = 39 + dy if cn else 8 - dy
+                    for t in range(4):
+                        fields[f][x, t, y:y + 1, :] = got[2 * cw + cn, t, r:r + 1, :]
+
+    def send_corners(corner, got_corner):
+        copies = []
         for dw, dn in CORNERS:
-            side, pairs = (dn + 1) // 2, pl.ds(0 if dw < 0 else 6, 2)
-            there_w, there_n = (1 - dw) // 2, (1 - dn) // 2
-            copies.append(remote(packed.at[side, :, pairs], got_corner.at[2 * there_w + there_n], dw, dn))
+            here = (dw + 1) + (dn + 1) // 2
+            copies.append(remote(corner.at[here], got_corner.at[3 - here], dw, dn))
         return copies
 
-    def unpack(field, got, got_corner, which):
+    def send_rows(packed, got):
+        return [remote(packed.at[0], got.at[1], 0, -1), remote(packed.at[1], got.at[0], 0, 1)]
+
+    def unpack(field, got, which):
         def place(x, t, half, lower, upper):
             field[x, t, 4:8, :] = lower[4 * half:4 * half + 4]
             field[x, t, 40:44, :] = upper[4 * half:4 * half + 4]
@@ -296,13 +332,6 @@
             return 0
 
         lax.fori_loop(0, 8, body, 0)
-        for there_w in (0, 1):
-            for p in range(2):
-                for t in range(4):
-                    lower = got_corner[2 * there_w, which, p, t]
-                    upper = got_corner[2 * there_w + 1, which, p, t]
-                    for half in (0, 1):
-                        place((22 if there_w else 2) + 2 * p + half, t, half, lower, upper)
 
     def unpack_fifth(field, got5):
         for x in range(16):
@@ -310,16 +339,29 @@
                 field[6 + x, t, 3:4, :] = got5[0, t, x:x + 1, :]
                 field[6 + x, t, 44:45, :] = got5[1, t, x:x + 1, :]
 
+    loads[0].wait()
+    to_split(lambda x, r, a: cf[0, x, 8 * r:8 * r + 8, 128 * a:128 * a + 128], tb)
+    pl.semaphore_wait(barrier, len(GREETED))
+    round0_coef = send_planes(tb, 5)
+    pack(tb, pk, 2)
+    round0_coef += send_rows(pk.at[:, 2], py.at[:, 2])
+    pack_fifth(tb, pk5)
+    round0_coef += send_rows(pk5, py5)
+    loads[1].wait()
+    to_split(lambda x, r, a: cf[1, x, 8 * r:8 * r + 8, 128 * a:128 * a + 128], tc)
+    round0_coef += send_planes(tc, 4)
+    pack(tc, pk, 1)
+    round0_coef += send_rows(pk.at[:, 1], py.at[:, 1])
+    pack_corners((tb, tc), CORNER_BC, pkc)
+    round0_coef += send_corners(pkc, pc)
+    loads[2].wait()
+    to_split(lambda x, r, a: rhs[x, 8 * r:8 * r + 8, 128 * a:128 * a + 128], ts)
+    round0_src = send_planes(ts, 4)
     pack(ts, pk, 0)
-    pack(tc, pk, 1)
-    pack(tb, pk, 2)
-    pack_fifth(tb, pk5)
-
-    pl.semaphore_wait(barrier, len(LOW_SENDS))
-
-    round0 = send_planes(tb, 5) + send_planes(tc, 4) + send_planes(ts, 4)
-    round0 += send_rows(pk, pk5, py, py5, pc)
-    everything += round0
+    round0_src += send_rows(pk.at[:, 0], py.at[:, 0])
+    pack_corners((ts,), CORNER_S, pkcs)
+    round0_src += send_corners(pkcs, pcs)
+    round0 = round0_coef + round0_src
 
     index2, block2 = split_index(2)
 
@@ -331,50 +373,42 @@
                     mt[which, 8 + x, t, 8 + 8 * r:16 + 8 * r, :] = tile
         return 0
 
+    loads[3].wait()
     lax.fori_loop(0, 8, split_mid, 0)
-
-    def mid_slices(dw, dn):
-        planes = pl.ds(8, 8)
-        planes_there = pl.ds(8 - 8 * dw, 8)
+    loads[4].wait()
+    for which in (0, 1):
+        for x in range(4):
+            lc[which, 16 + 4 * core + x, n] = cl[which, x]
+
+    def mid_slices(dw, dn, depth=8):
+        depth = 8 if dw == 0 else depth
+        planes = pl.ds(16 - depth if dw > 0 else 8, depth)
+        planes_there = pl.ds(8 if dw == 0 else 16 if dw < 0 else 8 - depth, depth)
         rows = pl.ds(8, 16) if dn == 0 else pl.ds(8 if dn < 0 else 16, 8)
         rows_there = pl.ds(8, 16) if dn == 0 else pl.ds(24 if dn < 0 else 0, 8)
         return planes, rows, planes_there, rows_there
 
-    def send_mid(field, pair):
+    def send_mid(field, depth):
         copies = []
         for dw, dn in SIDES + CORNERS:
-            planes, rows, planes_there, rows_there = mid_slices(dw, dn)
-            if pair:
-                src = field.at[:, planes, :, rows]
-                dst = field.at[:, planes_there, :, rows_there]
-            else:
-                src = field.at[planes, :, rows]
-                dst = field.at[planes_there, :, rows_there]
-            copies.append(remote(src, dst, dw, dn))
+            planes, rows, planes_there, rows_there = mid_slices(dw, dn, depth)
+            copies.append(remote(field.at[planes, :, rows], field.at[planes_there, :, rows_there], dw, dn))
         return copies
 
-    mid_coef_copies = send_mid(mt, True)
-    everything += mid_coef_copies
-
     def send_low(src, dst_of):
-        return [remote(src, dst_of(4 - dw), dw, dn) for dw, dn in LOW_SENDS]
-
-    low_coef_copies = send_low(cl, lambda slot: lc.at[:, pl.ds(4 * slot, 4), n])
-    everything += low_coef_copies
-    for which in (0, 1):
-        for x in range(4):
-            lc[which, 16 + x, n] = cl[which, x]
-
-    landed(round0)
-    for which, field in enumerate((ts, tc, tb)):
-        unpack(field, py, pc, which)
+        return [remote(src, dst_of(4 - dw + core), dw, dn) for dw, dn in LOW_SENDS]
+
+    landed(round0_coef)
+    unpack(tb, py, 2)
+    unpack(tc, py, 1)
     unpack_fifth(tb, py5)
+    unpack_corners((tb, tc), CORNER_BC, pc)
 
     row_lo = lambda rows: jnp.where(n == 0, rows, 0)
     row_hi = lambda edge, last: jnp.where(n == NN - 1, edge, last)
     first_box, last_box = w == 0, w == NW - 1
 
-    fine = Level(6, 4, fh, ffx, ffy, ffz, frinv, fdiag, fsrc, fv)
+    fine = Level(6, 4, fh, ffx, ffy, ffz, frinv, fdiag, fsrc, (fv0, fv1))
     fine.setup(
         lambda x, j, t: tb[x, t, pl.ds(j, 8, stride=6), :],
         lambda x, j, t: tc[x, t, pl.ds(j, 8, stride=6), :],
@@ -382,6 +416,20 @@
         jnp.where(first_box, 6, -1), jnp.where(last_box, 22, 99),
         row_lo(8), row_hi(40, 48))
 
+    landed(round0_src)
+
+    coef_rows = []
+    for dn in (-1, 1):
+        planes, rows, _, rows_there = mid_slices(0, dn)
+        coef_rows.append(remote(mt.at[:, planes, :, rows], mt.at[:, planes, :, rows_there], 0, dn))
+    for dn in (1, 3, 2):
+        mine = lc.at[:, pl.ds(16 + 4 * core, 4), n]
+        coef_rows.append(remote(mine, mine, 0, dn))
+    everything += coef_rows
+
+    unpack(ts, py, 0)
+    unpack_corners((ts,), CORNER_S, pcs)
+
     def load_fine(x, _):
         for j in range(6):
             for t in range(4):
@@ -391,6 +439,19 @@
     lax.fori_loop(2, 26, load_fine, 0)
     fine.start(2, 24)
     fine.half_sweep(1, 3, 22)
+
+    landed(coef_rows)
+    mid_coef_copies = [
+        remote(mt.at[:, pl.ds(8, 7)], mt.at[:, pl.ds(16, 7)], -1, 0),
+        remote(mt.at[:, pl.ds(9, 7)], mt.at[:, pl.ds(1, 7)], 1, 0)]
+
+    def send_low_coef(dw, rows):
+        src = lc.at[:, pl.ds(16 + 4 * core, 4), rows]
+        return remote(src, lc.at[:, pl.ds(4 * (4 - dw + core), 4), rows], dw, 0)
+
+    low_coef_near = [send_low_coef(dw, pl.ds(0, 4)) for dw in (-2, 2)]
+    everything += mid_coef_copies + low_coef_near
+
     fine.half_sweep(0, 4, 20)
     fine.half_sweep(1, 5, 18)
 
@@ -403,23 +464,12 @@
 
     lax.fori_loop(0, 8, restrict_fine, 0)
 
-    round1 = send_mid(st, False)
-    everything += round1
-
-    def store_fine(x, _):
-        for j in range(6):
-            for t in range(4):
-                tv[x, t, pl.ds(j, 8, stride=6), :] = fv[x, j, t]
-        return 0
-
-    lax.fori_loop(6, 22, store_fine, 0)
-    pack(tv, pkv, 0)
-    pack_fifth(tv, pkv5)
-    fine_copies = send_planes(tv, 5) + send_rows(pkv, pkv5, pyv, pyv5, pcv)
-    everything += fine_copies
+    round1 = send_mid(st, 6)
+    low_coef_far = [send_low_coef(dw, pl.ds(n // 2, 3)) for dw in (-4, 4)]
+    everything += round1 + low_coef_far
 
     landed(mid_coef_copies)
-    mid = Level(4, 2, mh, mfx, mfy, mfz, mrinv, mdiag, msrc, mv)
+    mid = Level(4, 2, mh, mfx, mfy, mfz, mrinv, mdiag, msrc, (mv0, mv1))
     mid.setup(
         lambda x, j, t: mt[0, x, t, pl.ds(j, 8, stride=4), :],
         lambda x, j, t: mt[1, x, t, pl.ds(j, 8, stride=4), :],
@@ -446,36 +496,73 @@
             lstage[i, pl.ds(j, 8, stride=2), :] = value
         value = lstage[i, 4:12, :]
         s2own[i] = value
-        s2g[16 + i, n] = value
+        s2g[16 + 4 * core + i, n] = value
         return 0
 
     lax.fori_loop(0, 4, restrict_mid, 0)
+
+    def to_sibling(refs_of, boxes):
+        copies = []
+        for box in boxes:
+            part = refs_of(pl.ds(8 * box + 4 * core, 4))
+            k = count[0]
+            count[0] += 1
+            copy = pltpu.make_async_remote_copy(
+                src_ref=part, dst_ref=part, send_sem=send.at[k], recv_sem=recv.at[k],
+                device_id=(w + 1 - 2 * core, n), device_id_type=MESH)
+            copy.start()
+            copies.append(copy)
+        return copies
+
+    landed(low_coef_near + low_coef_far)
+    low_coef_shared = to_sibling(lambda planes: lc.at[:, planes], range(5))
+    everything += low_coef_shared
 
     round2 = send_low(s2own, lambda slot: s2g.at[pl.ds(4 * slot, 4), n])
     everything += round2
 
-    def store_mid(x, _):
-        for j in range(4):
+    def store_mid(q, _):
+        for half in (0, 1):
+            x = 2 * q + half
+            get = mid.reader(8 + x, half)
+            for j in range(4):
+                for t in range(2):
+                    mstage[x, t, pl.ds(j, 8, stride=4), :] = get(j, t)
             for t in range(2):
-                mstage[x, t, pl.ds(j, 8, stride=4), :] = mv[8 + x, j, t]
-        for t in range(2):
-            vt[8 + x, t, 8:24, :] = mstage[x, t, 8:24, :]
-        return 0
-
-    lax.fori_loop(0, 8, store_mid, 0)
-    mid_copies = send_mid(vt, False)
+                vt[8 + x, t, 8:24, :] = mstage[x, t, 8:24, :]
+        return 0
+
+    lax.fori_loop(0, 4, store_mid, 0)
+    mid_copies = send_mid(vt, 8)
     everything += mid_copies
 
-    landed(low_coef_copies)
+    def store_fine(q, _):
+        for half in (0, 1):
+            x = 6 + 2 * q + half
+            get = fine.reader(x, half)
+            for j in range(6):
+                for t in range(4):
+                    tv[x, t, pl.ds(j, 8, stride=6), :] = get(j, t)
+        return 0
+
+    lax.fori_loop(0, 8, store_fine, 0)
+    pack(tv, pkv, 0)
+    pack_fifth(tv, pkv5)
+    pack_corners((tv,), CORNER_V, pkvc)
+    fine_copies = send_planes(tv, 5) + send_rows(pkv.at[:, 0], pyv.at[:, 0]) + send_rows(pkv5, pyv5)
+    fine_copies += send_corners(pkvc, pcv)
+    everything += fine_copies
+
+    landed(low_coef_shared)
     lane, sub = iota(1), iota(0)
     par = (lane + sub) % 2 == 0
     zero = jnp.zeros((8, 128), F32)
-    low_lo = 16 - 4 * w
-    low_hi = 16 + 4 * (NW - w)
+    low_lo = 16 - 4 * (w - core)
+    low_hi = low_lo + 4 * NW
 
     for r in range(4):
         lh[0, r] = zero
-        lh[37, r] = zero
+        lh[41, r] = zero
 
     def fill_low(i, _):
         scale = jnp.where((i >= low_lo) & (i < low_hi), 0.5, 0.0).astype(F32)
@@ -483,12 +570,13 @@
             lh[1 + i, r] = lc[0, i, r] * scale
         return 0
 
-    lax.fori_loop(0, 36, fill_low, 0)
+    lax.fori_loop(0, 40, fill_low, 0, unroll=4)
 
     def open_low(i):
         return jnp.where((i == low_lo) | (i == low_hi), 0.0, 1.0).astype(F32)
 
-    def build_low(p, _):
+    def build_low(q, _):
+        p = q + 2 * core
         i = 2 * p
         edge_lo, edge_hi = open_low(i), open_low(i + 2)
         h = [[lh[i + k, r] for r in range(4)] for k in range(4)]
@@ -522,35 +610,47 @@
 
     lax.fori_loop(0, 18, build_low, 0)
 
-    landed(round2)
-
-    def load_low(p, _):
+    landed([copy for copy, (dw, dn) in zip(round2, LOW_SENDS) if abs(dw) < 4])
+    source_shared = to_sibling(lambda planes: s2g.at[planes], (1, 2, 3))
+    landed([copy for copy, (dw, dn) in zip(round2, LOW_SENDS) if abs(dw) == 4])
+    source_shared += to_sibling(lambda planes: s2g.at[planes], (0, 4))
+    everything += source_shared
+    landed(source_shared)
+
+    def load_low(q, _):
+        p = q + 2 * core
         for r in range(4):
             a, b = s2g[2 * p, r], s2g[2 * p + 1, r]
             lsrc[0, p, r] = jnp.where(par, a, b)
             lsrc[1, p, r] = jnp.where(par, b, a)
-            lv[0, p, r] = lsrc[0, p, r] * lcoef[p, r, 0, 6]
-        return 0
-
-    lax.fori_loop(0, 18, load_low, 0)
+            lv0[p, r] = lsrc[0, p, r] * lcoef[p, r, 0, 6]
+        return 0
+
+    lax.fori_loop(0, 18, load_low, 0, unroll=2)
 
     def low_half_sweep(colour, first, last):
-        def body(p, _):
-            other = [lv[1 - colour, p, r] for r in range(4)]
-            downs = [down(value) for value in other]
-            ups = [up(value) for value in other]
-            for r in range(4):
-                coef = lambda k: lcoef[p, r, colour, k]
-                before, after = lv[1 - colour, p - 1, r], lv[1 - colour, p + 1, r]
-                out = jnp.where(par, before, after) if colour == 0 else jnp.where(par, after, before)
-                total = lsrc[colour, p, r] + coef(0) * other[r] + coef(1) * out
-                total += coef(2) * jnp.where(sub == 0, downs[r - 1], downs[r])
-                total += coef(3) * jnp.where(sub == 7, ups[(r + 1) % 4], ups[r])
-                total += coef(4) * left(other[r]) + coef(5) * right(other[r])
-                lv[colour, p, r] = total * coef(6)
+        here, there = (lv0, lv1) if colour == 0 else (lv1, lv0)
+
+        def body(q, _):
+            first_pair = first + 2 * q + 2 * core
+            seen = [[there[first_pair + k, r] for r in range(4)] for k in (-1, 0, 1, 2)]
+            for k in (0, 1):
+                p = first_pair + k
+                before, other, after = seen[k:k + 3]
+                downs = [down(value) for value in other]
+                ups = [up(value) for value in other]
+                for r in range(4):
+                    coef = lambda which: lcoef[p, r, colour, which]
+                    a, b = (before, after) if colour == 0 else (after, before)
+                    total = lsrc[colour, p, r] + coef(0) * other[r] + coef(1) * jnp.where(par, a[r], b[r])
+                    total += coef(2) * jnp.where(sub == 0, downs[r - 1], downs[r])
+                    total += coef(3) * jnp.where(sub == 7, ups[(r + 1) % 4], ups[r])
+                    total += coef(4) * left(other[r]) + coef(5) * right(other[r])
+                    here[p, r] = total * coef(6)
             return 0
 
-        lax.fori_loop(first, last + 1, body, 0)
+        steps = (last + 1 - first) // 2
+        lax.fori_loop(0, steps, body, 0, unroll=2 if steps % 2 == 0 else 3 if steps % 3 == 0 else 1)
 
     for k in range(2, 13):
         low_half_sweep((k + 1) % 2, k // 2, 17 - k // 2)
@@ -560,7 +660,7 @@
         v2t[i, 40:48, :] = zero
     for p in range(6):
         for r in range(4):
-            a, b = lv[0, 6 + p, r], lv[1, 6 + p, r]
+            a, b = lv0[6 + 2 * core + p, r], lv1[6 + 2 * core + p, r]
             v2t[2 * p, 8 + 8 * r:16 + 8 * r, :] = jnp.where(par, a, b)
             v2t[2 * p + 1, 8 + 8 * r:16 + 8 * r, :] = jnp.where(par, b, a)
 
@@ -572,7 +672,8 @@
             for half in (0, 1):
                 for t in range(2):
                     x = 2 * i + half
-                    mv[x, j, t] = vt[x, t, pl.ds(j, 8, stride=4), :] + coarse
+                    if (half + j + t) % 2 == 1:
+                        mv1[x, j, t // 2] = vt[x, t, pl.ds(j, 8, stride=4), :] + coarse
         return 0
 
     lax.fori_loop(0, 12, correct_mid, 0)
@@ -581,17 +682,21 @@
     mid.half_sweep(0, 4, 16)
     mid.half_sweep(1, 5, 14)
 
-    def spread_mid(x, _):
-        for j in range(4):
-            for t in range(2):
-                vp[x, t, pl.ds(j, 8, stride=4), :] = mv[x, j, t]
-        return 0
-
-    lax.fori_loop(5, 19, spread_mid, 0)
+    def spread_mid(q, _):
+        for half in (0, 1):
+            x = 5 + 2 * q + half
+            get = mid.reader(x, 1 - half)
+            for j in range(4):
+                for t in range(2):
+                    vp[x, t, pl.ds(j, 8, stride=4), :] = get(j, t)
+        return 0
+
+    lax.fori_loop(0, 7, spread_mid, 0)
 
     landed(fine_copies)
-    unpack(tv, pyv, pcv, 0)
+    unpack(tv, pyv, 0)
     unpack_fifth(tv, pyv5)
+    unpack_corners((tv,), CORNER_V, pcv)
 
     def correct_fine(q, _):
         for j in range(3):
@@ -602,7 +707,7 @@
                     for jj in (2 * j, 2 * j + 1):
                         for tt in (2 * t, 2 * t + 1):
                             if (half + jj + tt) % 2 == 1:
-                                fv[x, jj, tt] = tv[x, tt, pl.ds(jj, 8, stride=6), :] + coarse
+                                fv1[x, jj, tt // 2] = tv[x, tt, pl.ds(jj, 8, stride=6), :] + coarse
         return 0
 
     lax.fori_loop(0, 14, correct_fine, 0)
@@ -611,27 +716,58 @@
     fine.half_sweep(0, 4, 20)
     fine.half_sweep(1, 5, 18)
 
-    join4, join_block4 = join_index(4)
-
-    def finish(x, _):
-        get = fine.reader(6 + x)
-        for j in range(6):
-            for t in range(4):
-                stage[0, t, pl.ds(j, 8, stride=6), :] = get(j, t)
-                stage[1, t, pl.ds(j, 8, stride=6), :] = fine.residual(6 + x, j, t, get)
-        for k, out in enumerate((out_v, out_r)):
-            for r in range(4):
-                tiles = [stage[k, t, 8 + 8 * r:16 + 8 * r, :] for t in range(4)]
-                for a, part in enumerate(join_lanes(tiles, join4, join_block4)):
-                    out[x, 8 * r:8 * r + 8, 128 * a:128 * a + 128] = part
-        return 0
-
-    lax.fori_loop(0, 16, finish, 0)
+    for copy in round0:
+        copy.wait_send()
+
+    def result(k, x):
+        staged, hbm = ((ts, hbm_v), (tc, hbm_r))[k]
+        return pltpu.make_async_copy(staged.at[6 + x, :, pl.ds(8, 32)], hbm.at[x], out_sem.at[k, x])
+
+    def finish(q, _):
+        for half in (0, 1):
+            x = 2 * q + half
+            get = fine.reader(6 + x, half)
+            for j in range(6):
+                for t in range(4):
+                    ts[6 + x, t, pl.ds(j, 8, stride=6), :] = get(j, t)
+                    tc[6 + x, t, pl.ds(j, 8, stride=6), :] = fine.residual(6 + x, half, j, t, get)
+            result(0, x).start()
+            result(1, x).start()
+        return 0
+
+    def settle(x, _):
+        result(0, x).wait()
+        result(1, x).wait()
+        return 0
+
+    lax.fori_loop(0, 8, finish, 0)
+    lax.fori_loop(0, 16, settle, 0)
     for copy in everything:
         copy.wait_send()
 
 
-N_COPIES = 14 + 8 + 35 + 8 + 10 + 35 + 8
+def join_kernel(v_ref, r_ref, out_v, out_r):
+    index, block = join_index(4)
+    for tiles_ref, out in ((v_ref, out_v), (r_ref, out_r)):
+        for x in range(tiles_ref.shape[0]):
+            for r in range(4):
+                tiles = [tiles_ref[x, t, 8 * r:8 * r + 8, :] for t in range(4)]
+                for a, part in enumerate(join_lanes(tiles, index, block)):
+                    out[x, 8 * r:8 * r + 8, 128 * a:128 * a + 128] = part
+
+
+def join(v, r):
+    shape = jax.ShapeDtypeStruct((16, 32, 512), F32)
+    tiles = pl.BlockSpec((4, 4, 32, 128), lambda i: (i, 0, 0, 0))
+    whole = pl.BlockSpec((4, 32, 512), lambda i: (i, 0, 0))
+    return pl.pallas_call(
+        join_kernel, grid=(4,), out_shape=(shape, shape),
+        in_specs=[tiles] * 2, out_specs=(whole, whole),
+        compiler_params=pltpu.CompilerParams(vmem_limit_bytes=16 * 2**20),
+    )(v, r)
+
+
+N_COPIES = 14 + 8 + 5 + 6 + 8 + 10 + 5 + 17 + 8 + 5
 
 
 def vmem(*shape):
@@ -639,33 +775,35 @@
 
 
 def v_cycle(rhs, cf, cm, cl):
-    vm = pl.BlockSpec(memory_space=pltpu.VMEM)
-    shape = jax.ShapeDtypeStruct(rhs.shape, F32)
+    hbm = pl.BlockSpec(memory_space=pl.ANY)
+    shape = jax.ShapeDtypeStruct((16, 4, 32, 128), F32)
     fine_t = (28, 4, 48, 128)
     fine_a = (28, 6, 4, 8, 128)
     mid_t = (24, 2, 32, 128)
     mid_a = (24, 4, 2, 8, 128)
     scratch = [
+        vmem(*rhs.shape), vmem(*cf.shape), vmem(*cm.shape), vmem(*cl.shape),
+        pltpu.SemaphoreType.DMA((5,)), pltpu.SemaphoreType.DMA((2, 16)),
         vmem(*fine_t), vmem(*fine_t), vmem(*fine_t), vmem(*fine_t),
-        vmem(2, 3, 8, 4, 8, 128), vmem(2, 4, 16, 128),
-        vmem(2, 3, 8, 4, 8, 128), vmem(2, 4, 16, 128), vmem(4, 3, 2, 4, 8, 128),
+        vmem(2, 3, 8, 4, 8, 128), vmem(2, 4, 16, 128), vmem(4, 4, 16, 128), vmem(4, 4, 8, 128),
+        vmem(2, 3, 8, 4, 8, 128), vmem(2, 4, 16, 128), vmem(4, 4, 16, 128), vmem(4, 4, 8, 128),
         vmem(*fine_a), vmem(*fine_a), vmem(28, 7, 4, 8, 128), vmem(28, 6, 5, 8, 128),
-        vmem(*fine_a), vmem(*fine_a), vmem(*fine_a), vmem(*fine_a), vmem(2, 4, 48, 128),
+        vmem(*fine_a), vmem(*fine_a), vmem(*fine_a), vmem(28, 6, 2, 8, 128), vmem(28, 6, 2, 8, 128),
         vmem(2, *mid_t), vmem(*mid_t), vmem(*mid_t), vmem(*mid_t),
         vmem(*mid_a), vmem(*mid_a), vmem(24, 5, 2, 8, 128), vmem(24, 4, 3, 8, 128),
-        vmem(*mid_a), vmem(*mid_a), vmem(*mid_a), vmem(*mid_a),
+        vmem(*mid_a), vmem(*mid_a), vmem(*mid_a), vmem(24, 4, 1, 8, 128), vmem(24, 4, 1, 8, 128),
         vmem(8, 2, 32, 128), vmem(4, 16, 128),
-        vmem(2, 36, 4, 8, 128), vmem(4, 8, 128), vmem(36, 4, 8, 128), vmem(38, 4, 8, 128),
-        vmem(18, 4, 2, 7, 8, 128), vmem(2, 18, 4, 8, 128), vmem(2, 18, 4, 8, 128), vmem(12, 48, 128),
-        vmem(2, 1, 8, 4, 8, 128), vmem(2, 4, 16, 128),
-        vmem(2, 1, 8, 4, 8, 128), vmem(2, 4, 16, 128), vmem(4, 1, 2, 4, 8, 128),
+        vmem(2, 40, 4, 8, 128), vmem(4, 8, 128), vmem(40, 4, 8, 128), vmem(42, 4, 8, 128),
+        vmem(20, 4, 2, 7, 8, 128), vmem(2, 20, 4, 8, 128), vmem(20, 4, 8, 128), vmem(20, 4, 8, 128), vmem(12, 48, 128),
+        vmem(2, 1, 8, 4, 8, 128), vmem(2, 4, 16, 128), vmem(4, 4, 16, 128),
+        vmem(2, 1, 8, 4, 8, 128), vmem(2, 4, 16, 128), vmem(4, 4, 16, 128),
         pltpu.SemaphoreType.DMA((N_COPIES,)), pltpu.SemaphoreType.DMA((N_COPIES,)),
     ]
     return pl.pallas_call(
         kernel,
         out_shape=(shape, shape),
-        in_specs=[vm] * 4,
-        out_specs=(vm, vm),
+        in_specs=[hbm] * 4,
+        out_specs=(hbm, hbm),
         scratch_shapes=scratch,
         compiler_params=pltpu.CompilerParams(
             collective_id=0, has_side_effects=True, vmem_limit_bytes=60 * 2**20),
@@ -678,7 +816,7 @@
         return lambda a, b: (lax.ppermute(a, "wide", pairs), lax.ppermute(b, "wide", pairs))
 
     cm, cl = lax.switch(offset[0] - 1, [moved(k) for k in range(1, NW)], cm, cl)
-    return v_cycle(rhs, cf, cm, cl)
+    return join(*v_cycle(rhs, cf, cm, cl))
 
 
 def solution(mesh):

time: 134 us -> 104 us (0.78)
  Pallas kernels: 103 us -> 88.2 us
  starting transfers between devices: 19.6 us -> 5.02 us
    pallas_call x1 -> x2, Pallas kernels: 103 us -> 88.2 us  [the longest x1 80.4 us: v_cycle(): pl.pallas_call(kernel, out_shape=(shape, shape), in_specs=[hbm] * 4, out_...]
    ppermute x1, starting transfers between devices: 8.9 us -> 1.39 us  [moved(): lax.ppermute(b, 'wide', pairs)]
    ppermute x1, starting transfers between devices: 10.7 us -> 3.63 us  [moved(): lax.ppermute(a, 'wide', pairs)]
where the time goes in v2:
time: 104 us; the launch traced here: 103 us
  Pallas kernels  88.2 us (85%)
  waiting for transfers between devices  6.11 us (6%)
  starting transfers between devices  5.02 us (5%)
  local copies, waits for them, and re-layouts  2.44 us (2%)
  between operations  1.3 us (1%)
    pallas_call x1, Pallas kernels, v_cycle(): pl.pallas_call(kernel, out_shape=(shape, shape), in_specs=[hbm] * 4, out_...  80.4 us
    pallas_call x1, Pallas kernels, join(): pl.pallas_call(join_kernel, grid=(4,), out_shape=(shape, shape), in_specs...  7.79 us
    ppermute x1, waiting for transfers between devices, moved(): lax.ppermute(b, 'wide', pairs)  6.1 us
    ppermute x1, starting transfers between devices, moved(): lax.ppermute(a, 'wide', pairs)  3.63 us
    unnamed x4, local copies, waits for them, and re-layouts  2.44 us
  transfers between devices with their start and end apart: 2, of which 1 were waited for; matrix products, arithmetic and copies ran while one was open for 0% of the time, Pallas kernels for 0%

profile of v2, /device:TPU:1, one launch (start us, length us, event | category | flops | bytes accessed | tf_op | source)
XLA Modules:
  0.0 103.3 jit_solution(4037508632182826640)
XLA Ops:
  1.3 11.4 %conditional.1 = (f32[2,8,16,256]{3,2,1,0:T(8,128)}, f32[2,4,8,128]{3,2,1,0:T(8,128)}) conditional(s32[]{:T(128)} %bitcast, (f32[2,8,16,256]{3,2,1,0:T(8,128)}, f32[2,4,8,128]{3,2,1,0:T(8,128)}) %tuple.131, (f32[2,8,16,256]{3,2,1,0:T(8,128)}, f32[2,4,8,128]{3,2,1,0:T(8,128)}) %tuple.131, ...), branch_computations={%region_0.0_spmd, %region_1.0_spmd, %region_2.0_spmd, %region_3.0_... | conditional | bytes 1179744 | solution.py:818
  1.5 3.6 %collective-permute-start.50 = (f32[2,8,16,256]{3,2,1,0:T(8,128)}, f32[2,8,16,256]{3,2,1,0:T(8,128)}, u32[]{:S(2)}, u32[]{:S(2)}) collective-permute-start(f32[2,8,16,256]{3,2,1,0:T(8,128)} %get-tuple-element.174), channel_id=1, source_target_pairs={{104,0},{108,4},{112,8},{116,12},{120,16},{124,20},{0,24},{4,28},{... | collective-permute-start | bytes 786440 | tf_op jit(solution)/shard_map/cond/branch_25_fun/ppermute | solution.py:816
  5.2 1.4 %collective-permute-start.51 = (f32[2,4,8,128]{3,2,1,0:T(8,128)}, f32[2,4,8,128]{3,2,1,0:T(8,128)}, u32[]{:S(2)}, u32[]{:S(2)}) collective-permute-start(f32[2,4,8,128]{3,2,1,0:T(8,128)} %get-tuple-element.175), channel_id=1, source_target_pairs={{104,0},{108,4},{112,8},{116,12},{120,16},{124,20},{0,24},{4,28},{... | collective-permute-start | bytes 98312 | tf_op jit(solution)/shard_map/cond/branch_25_fun/ppermute | solution.py:816
  6.6 6.1 %collective-permute-done.51 = f32[2,4,8,128]{3,2,1,0:T(8,128)} collective-permute-done((f32[2,4,8,128]{3,2,1,0:T(8,128)}, f32[2,4,8,128]{3,2,1,0:T(8,128)}, u32[]{:S(2)}, u32[]{:S(2)}) %collective-permute-start.51) | collective-permute-done | bytes 32800 | tf_op jit(solution)/shard_map/cond/branch_25_fun/ppermute | solution.py:816
  12.7 0.0 collective-permute-done.50
  12.7 80.4 %shard_map.68 = (f32[16,4,32,128]{3,2,1,0:T(8,128)}, f32[16,4,32,128]{3,2,1,0:T(8,128)}) custom-call(f32[16,32,512]{2,1,0:T(8,128)} %rhs_hbm.1, f32[2,16,32,512]{3,2,1,0:T(8,128)} %cf_hbm.1, f32[2,8,16,256]{3,2,1,0:T(8,128)} %get-tuple-element.192.cm_hbm, f32[2,4,8,128]{3,2,1,0:T(8,128)} %get-tuple-element.193.cl_hbm), custom_call_target="tpu_custom_call" | custom-call | tf_op jit(solution)/shard_map/pallas_call | solution.py:802
  93.1 0.0 copy-start
  93.1 1.2 %copy-done = f32[16,4,32,128]{3,2,1,0:T(8,128)S(1)} copy-done((f32[16,4,32,128]{3,2,1,0:T(8,128)S(1)}, f32[16,4,32,128]{3,2,1,0:T(8,128)}, u32[]{:S(2)}) %copy-start) | copy-done | bytes 1048600
  94.3 0.0 copy-start.1
  94.3 1.2 %copy-done.1 = f32[16,4,32,128]{3,2,1,0:T(8,128)S(1)} copy-done((f32[16,4,32,128]{3,2,1,0:T(8,128)S(1)}, f32[16,4,32,128]{3,2,1,0:T(8,128)}, u32[]{:S(2)}) %copy-start.1) | copy-done | bytes 1048600
  95.6 7.8 %shard_map.69 = (f32[16,32,512]{2,1,0:T(8,128)}, f32[16,32,512]{2,1,0:T(8,128)}) custom-call(f32[16,4,32,128]{3,2,1,0:T(8,128)S(1)} %copy-done, f32[16,4,32,128]{3,2,1,0:T(8,128)S(1)} %copy-done.1), custom_call_target="tpu_custom_call" | custom-call | tf_op jit(solution)/shard_map/pallas_call | solution.py:763
Async XLA Ops:
  1.5 11.1 %collective-permute-start.50 = (f32[2,8,16,256]{3,2,1,0:T(8,128)}, f32[2,8,16,256]{3,2,1,0:T(8,128)}, u32[]{:S(2)}, u32[]{:S(2)}) collective-permute-start(f32[2,8,16,256]{3,2,1,0:T(8,128)} %get-tuple-element.174), channel_id=1, source_target_pairs={{104,0},{108,4},{112,8},{116,12},{120,16},{124,20},{0,24},{4,28},{... | collective-permute-start | bytes 786440 | tf_op jit(solution)/shard_map/cond/branch_25_fun/ppermute | solution.py:816
  5.2 7.5 %collective-permute-start.51 = (f32[2,4,8,128]{3,2,1,0:T(8,128)}, f32[2,4,8,128]{3,2,1,0:T(8,128)}, u32[]{:S(2)}, u32[]{:S(2)}) collective-permute-start(f32[2,4,8,128]{3,2,1,0:T(8,128)} %get-tuple-element.175), channel_id=1, source_target_pairs={{104,0},{108,4},{112,8},{116,12},{120,16},{124,20},{0,24},{4,28},{... | collective-permute-start | bytes 98312 | tf_op jit(solution)/shard_map/cond/branch_25_fun/ppermute | solution.py:816
  93.1 1.2 %copy-start = (f32[16,4,32,128]{3,2,1,0:T(8,128)S(1)}, f32[16,4,32,128]{3,2,1,0:T(8,128)}, u32[]{:S(2)}) copy-start(f32[16,4,32,128]{3,2,1,0:T(8,128)} %get-tuple-element.194.v_ref) | copy-start | bytes 3145732
  94.3 1.2 %copy-start.1 = (f32[16,4,32,128]{3,2,1,0:T(8,128)S(1)}, f32[16,4,32,128]{3,2,1,0:T(8,128)}, u32[]{:S(2)}) copy-start(f32[16,4,32,128]{3,2,1,0:T(8,128)} %get-tuple-element.195.r_ref) | copy-start | bytes 3145732

commit v3 on v2

--- a/solution.py
+++ b/solution.py
@@ -1,3 +1,5 @@
+import functools
+
 import jax
 import jax.numpy as jnp
 from jax import lax
@@ -27,41 +29,30 @@
     return jnp.take_along_axis(x, index, axis=1, mode="promise_in_bounds")
 
 
-def split_index(n):
+def swap(first, second, bit):
+    low = iota(1) & bit == 0
+    return (jnp.where(low, first, pltpu.roll(second, bit, 1)),
+            jnp.where(low, pltpu.roll(first, 128 - bit, 1), second))
+
+
+def split_lanes(parts):
+    a, b = swap(parts[0], parts[1], 1)
+    c, d = swap(parts[2], parts[3], 1)
+    (a, c), (b, d) = swap(a, c, 2), swap(b, d, 2)
+    return [a, b, c, d]
+
+
+def join_lanes(tiles):
+    a, b, c, d = tiles
+    (a, c), (b, d) = swap(a, c, 2), swap(b, d, 2)
+    a, b = swap(a, b, 1)
+    c, d = swap(c, d, 1)
+    return [a, b, c, d]
+
+
+def place_index():
     lane = iota(1)
-    width = 128 // n
-    block, place = lane // width, lane % width
-    return [n * place + (block - a) % n for a in range(n)], block
-
-
-def split_lanes(parts, index, block):
-    n = len(parts)
-    gathered = [take(part, index[a]) for a, part in enumerate(parts)]
-    out = []
-    for t in range(n):
-        tile = gathered[(n - 1 - t) % n]
-        for place in range(n - 1):
-            tile = jnp.where(block == place, gathered[(place - t) % n], tile)
-        out.append(tile if t == 0 else pltpu.roll(tile, 128 - t * (128 // n), 1))
-    return out
-
-
-def join_index(n):
-    lane = iota(1)
-    width = 128 // n
-    return [width * ((lane % n + a) % n) + lane // n for a in range(n)], lane // width
-
-
-def join_lanes(tiles, index, block):
-    n = len(tiles)
-    turned = [tiles[t] if t == 0 else pltpu.roll(tiles[t], t * (128 // n), 1) for t in range(n)]
-    out = []
-    for a in range(n):
-        tile = turned[(n - 1 - a) % n]
-        for place in range(n - 1):
-            tile = jnp.where(block == place, turned[(place - a) % n], tile)
-        out.append(take(tile, index[a]))
-    return out
+    return 32 * (lane % 4) + lane // 4
 
 
 def down(x):
@@ -73,11 +64,11 @@
 
 
 def left(x):
-    return pltpu.roll(x, 1, 1)
+    return jnp.where(iota(1) < 4, pltpu.roll(x, 5, 1), pltpu.roll(x, 4, 1))
 
 
 def right(x):
-    return pltpu.roll(x, 127, 1)
+    return jnp.where(iota(1) >= 124, pltpu.roll(x, 123, 1), pltpu.roll(x, 124, 1))
 
 
 class Level:
@@ -255,13 +246,11 @@
 
     everything = []
 
-    index4, block4 = split_index(4)
-
     def to_split(read, target):
         def body(x, _):
             for r in range(4):
                 parts = [read(x, r, a) for a in range(4)]
-                for t, tile in enumerate(split_lanes(parts, index4, block4)):
+                for t, tile in enumerate(split_lanes(parts)):
                     target[6 + x, t, 8 + 8 * r:16 + 8 * r, :] = tile
             return 0
 
@@ -363,13 +352,15 @@
     round0_src += send_corners(pkcs, pcs)
     round0 = round0_coef + round0_src
 
-    index2, block2 = split_index(2)
+    place = place_index()
 
     def split_mid(x, _):
         for which in (0, 1):
             for r in range(2):
-                parts = [cm[which, x, 8 * r:8 * r + 8, 128 * a:128 * a + 128] for a in range(2)]
-                for t, tile in enumerate(split_lanes(parts, index2, block2)):
+                low, high = [cm[which, x, 8 * r:8 * r + 8, 128 * a:128 * a + 128] for a in range(2)]
+                for t in range(2):
+                    index = (2 * place + t) % 128
+                    tile = jnp.where(place < 64, take(low, index), take(high, index))
                     mt[which, 8 + x, t, 8 + 8 * r:16 + 8 * r, :] = tile
         return 0
 
@@ -378,7 +369,7 @@
     loads[4].wait()
     for which in (0, 1):
         for x in range(4):
-            lc[which, 16 + 4 * core + x, n] = cl[which, x]
+            lc[which, 16 + 4 * core + x, n] = take(cl[which, x], place)
 
     def mid_slices(dw, dn, depth=8):
         depth = 8 if dw == 0 else depth
@@ -399,6 +390,11 @@
         return [remote(src, dst_of(4 - dw + core), dw, dn) for dw, dn in LOW_SENDS]
 
     landed(round0_coef)
+    mid_coef_copies = []
+    for dw, dn in SIDES + CORNERS:
+        planes, rows, planes_there, rows_there = mid_slices(dw, dn, 7)
+        mid_coef_copies.append(remote(mt.at[:, planes, :, rows], mt.at[:, planes_there, :, rows_there], dw, dn))
+    everything += mid_coef_copies
     unpack(tb, py, 2)
     unpack(tc, py, 1)
     unpack_fifth(tb, py5)
@@ -419,9 +415,6 @@
     landed(round0_src)
 
     coef_rows = []
-    for dn in (-1, 1):
-        planes, rows, _, rows_there = mid_slices(0, dn)
-        coef_rows.append(remote(mt.at[:, planes, :, rows], mt.at[:, planes, :, rows_there], 0, dn))
     for dn in (1, 3, 2):
         mine = lc.at[:, pl.ds(16 + 4 * core, 4), n]
         coef_rows.append(remote(mine, mine, 0, dn))
@@ -441,16 +434,12 @@
     fine.half_sweep(1, 3, 22)
 
     landed(coef_rows)
-    mid_coef_copies = [
-        remote(mt.at[:, pl.ds(8, 7)], mt.at[:, pl.ds(16, 7)], -1, 0),
-        remote(mt.at[:, pl.ds(9, 7)], mt.at[:, pl.ds(1, 7)], 1, 0)]
-
     def send_low_coef(dw, rows):
         src = lc.at[:, pl.ds(16 + 4 * core, 4), rows]
         return remote(src, lc.at[:, pl.ds(4 * (4 - dw + core), 4), rows], dw, 0)
 
     low_coef_near = [send_low_coef(dw, pl.ds(0, 4)) for dw in (-2, 2)]
-    everything += mid_coef_copies + low_coef_near
+    everything += low_coef_near
 
     fine.half_sweep(0, 4, 20)
     fine.half_sweep(1, 5, 18)
@@ -555,7 +544,7 @@
 
     landed(low_coef_shared)
     lane, sub = iota(1), iota(0)
-    par = (lane + sub) % 2 == 0
+    par = (lane // 4 + sub) % 2 == 0
     zero = jnp.zeros((8, 128), F32)
     low_lo = 16 - 4 * (w - core)
     low_hi = low_lo + 4 * NW
@@ -747,27 +736,29 @@
 
 
 def join_kernel(v_ref, r_ref, out_v, out_r):
-    index, block = join_index(4)
-    for tiles_ref, out in ((v_ref, out_v), (r_ref, out_r)):
-        for x in range(tiles_ref.shape[0]):
+    def body(x, _):
+        for tiles_ref, out in ((v_ref, out_v), (r_ref, out_r)):
             for r in range(4):
                 tiles = [tiles_ref[x, t, 8 * r:8 * r + 8, :] for t in range(4)]
-                for a, part in enumerate(join_lanes(tiles, index, block)):
+                for a, part in enumerate(join_lanes(tiles)):
                     out[x, 8 * r:8 * r + 8, 128 * a:128 * a + 128] = part
+        return 0
+
+    lax.fori_loop(0, v_ref.shape[0], body, 0)
 
 
 def join(v, r):
     shape = jax.ShapeDtypeStruct((16, 32, 512), F32)
-    tiles = pl.BlockSpec((4, 4, 32, 128), lambda i: (i, 0, 0, 0))
-    whole = pl.BlockSpec((4, 32, 512), lambda i: (i, 0, 0))
+    tiles = pl.BlockSpec((8, 4, 32, 128), lambda i: (i, 0, 0, 0))
+    whole = pl.BlockSpec((8, 32, 512), lambda i: (i, 0, 0))
     return pl.pallas_call(
-        join_kernel, grid=(4,), out_shape=(shape, shape),
+        join_kernel, grid=(2,), out_shape=(shape, shape),
         in_specs=[tiles] * 2, out_specs=(whole, whole),
-        compiler_params=pltpu.CompilerParams(vmem_limit_bytes=16 * 2**20),
+        compiler_params=pltpu.CompilerParams(vmem_limit_bytes=60 * 2**20),
     )(v, r)
 
 
-N_COPIES = 14 + 8 + 5 + 6 + 8 + 10 + 5 + 17 + 8 + 5
+N_COPIES = 14 + 8 + 8 + 3 + 4 + 8 + 10 + 5 + 17 + 8 + 5
 
 
 def vmem(*shape):
@@ -810,10 +801,32 @@
     )(rhs, cf, cm, cl)
 
 
+def shift_kernel(k, cm, cl, out_m, out_l, send, recv):
+    w, n = lax.axis_index("wide"), lax.axis_index("narrow")
+    barrier = pltpu.get_barrier_semaphore()
+    pl.semaphore_signal(barrier, inc=1, device_id=(lax.rem(w + k, NW), n), device_id_type=MESH)
+    pl.semaphore_wait(barrier, 1)
+    copies = [
+        pltpu.make_async_remote_copy(
+            src_ref=src, dst_ref=dst, send_sem=send.at[i], recv_sem=recv.at[i],
+            device_id=(lax.rem(w + (NW - k), NW), n), device_id_type=MESH)
+        for i, (src, dst) in enumerate(((cm, out_m), (cl, out_l)))]
+    for copy in copies:
+        copy.start()
+    for copy in copies:
+        copy.wait()
+
+
 def on_device(rhs, cf, cm, cl, offset):
     def moved(k):
-        pairs = [((i + k) % NW, i) for i in range(NW)]
-        return lambda a, b: (lax.ppermute(a, "wide", pairs), lax.ppermute(b, "wide", pairs))
+        return lambda a, b: pl.pallas_call(
+            functools.partial(shift_kernel, k),
+            out_shape=(jax.ShapeDtypeStruct(a.shape, F32), jax.ShapeDtypeStruct(b.shape, F32)),
+            in_specs=[pl.BlockSpec(memory_space=pl.ANY)] * 2,
+            out_specs=(pl.BlockSpec(memory_space=pl.ANY),) * 2,
+            scratch_shapes=[pltpu.SemaphoreType.DMA((2,)), pltpu.SemaphoreType.DMA((2,))],
+            compiler_params=pltpu.CompilerParams(collective_id=k, has_side_effects=True),
+        )(a, b)
 
     cm, cl = lax.switch(offset[0] - 1, [moved(k) for k in range(1, NW)], cm, cl)
     return join(*v_cycle(rhs, cf, cm, cl))

time: 104 us -> 88.9 us (0.85)
  waiting for transfers between devices: 6.11 us -> 0 us
  starting transfers between devices: 5.02 us -> 0 us
  local copies, waits for them, and re-layouts: 2.44 us -> 0 us
    pallas_call x1, Pallas kernels: 80.4 us -> 70.3 us  [v_cycle(): pl.pallas_call(kernel, out_shape=(shape, shape), in_specs=[hbm] * 4, out_...]
    pallas_call x1 -> x2, Pallas kernels: 7.79 us -> 17.1 us  [the longest x1 12.1 us: moved(): pl.pallas_call(functools.partial(shift_kernel, k), out_shape=(jax.ShapeDt...]
    ppermute x2 -> x0, waiting for transfers between devices: 6.11 us -> none  [the longest x1 6.1 us: moved(): lax.ppermute(b, 'wide', pairs)]
    ppermute x2 -> x0, starting transfers between devices: 5.02 us -> none  [the longest x1 3.63 us: moved(): lax.ppermute(a, 'wide', pairs)]
    unnamed x4 -> x0, local copies, waits for them, and re-layouts: 2.44 us -> none
  transfers between devices with their start and end apart: 2 -> 0, of which waited for: 1 -> 0; matrix products, arithmetic and copies ran while one was open for 0% -> 0% of each run, Pallas kernels for 0% -> 0%
where the time goes in v3:
time: 88.9 us; the launch traced here: 88.8 us
  Pallas kernels  87.4 us (98%)
  between operations  1.29 us (1%)
    pallas_call x1, Pallas kernels, v_cycle(): pl.pallas_call(kernel, out_shape=(shape, shape), in_specs=[hbm] * 4, out_...  70.3 us
    pallas_call x1, Pallas kernels, moved(): pl.pallas_call(functools.partial(shift_kernel, k), out_shape=(jax.ShapeDt...  12.1 us
    pallas_call x1, Pallas kernels, join(): pl.pallas_call(join_kernel, grid=(2,), out_shape=(shape, shape), in_specs...  4.95 us

profile of v3, /device:TPU:1, one launch (start us, length us, event | category | flops | bytes accessed | tf_op | source)
XLA Modules:
  0.0 88.8 jit_solution(4438588031067370051)
XLA Ops:
  1.3 12.2 %conditional.1 = ((f32[2,8,16,256]{3,2,1,0:T(8,128)S(1)}, f32[2,4,8,128]{3,2,1,0:T(8,128)S(1)})) conditional(s32[]{:T(128)} %bitcast, (f32[2,8,16,256]{3,2,1,0:T(8,128)}, f32[2,4,8,128]{3,2,1,0:T(8,128)}) %tuple.100, (f32[2,8,16,256]{3,2,1,0:T(8,128)}, f32[2,4,8,128]{3,2,1,0:T(8,128)}) %tuple.100, ...), branch_computations={%region_0.0_spmd, %region_1.0_spmd, %region_2.0_spmd, %region_3.0_... | conditional | bytes 8 | solution.py:831
  1.3 12.1 %branch_9_fun.1 = (f32[2,8,16,256]{3,2,1,0:T(8,128)S(1)}, f32[2,4,8,128]{3,2,1,0:T(8,128)S(1)}) custom-call(f32[2,8,16,256]{3,2,1,0:T(8,128)} %get-tuple-element.142.cm, f32[2,4,8,128]{3,2,1,0:T(8,128)} %get-tuple-element.143.cl), custom_call_target="tpu_custom_call" | custom-call | tf_op jit(solution)/shard_map/cond/branch_9_fun/pallas_call | solution.py:822
  13.5 70.3 %shard_map.68 = (f32[16,4,32,128]{3,2,1,0:T(8,128)}, f32[16,4,32,128]{3,2,1,0:T(8,128)}) custom-call(f32[16,32,512]{2,1,0:T(8,128)} %rhs_hbm.1, f32[2,16,32,512]{3,2,1,0:T(8,128)} %cf_hbm.1, f32[2,8,16,256]{3,2,1,0:T(8,128)S(1)} %get-tuple-element.192.cm_hbm, f32[2,4,8,128]{3,2,1,0:T(8,128)S(1)} %get-tuple-element.193.cl_hbm), custom_call_target="tpu_custom_call" | custom-call | tf_op jit(solution)/shard_map/pallas_call | solution.py:793
  83.8 5.0 %shard_map.69 = (f32[16,32,512]{2,1,0:T(8,128)}, f32[16,32,512]{2,1,0:T(8,128)}) custom-call(f32[16,4,32,128]{3,2,1,0:T(8,128)} %get-tuple-element.194.v_ref, f32[16,4,32,128]{3,2,1,0:T(8,128)} %get-tuple-element.195.r_ref), custom_call_target="tpu_custom_call" | custom-call | tf_op jit(solution)/shard_map/pallas_call | solution.py:754

commit v4 on v3

--- a/solution.py
+++ b/solution.py
@@ -14,7 +14,7 @@
              if (dw, dn) not in ((0, 0), (-4, 2), (4, 2))]
 CORNERS = [(dw, dn) for dw in (-1, 1) for dn in (-1, 1)]
 SIDES = [(-1, 0), (1, 0), (0, -1), (0, 1)]
-GREETED = SIDES + CORNERS + [(-2, 0), (2, 0), (-4, 0), (4, 0)]
+GREETED = SIDES + CORNERS + [(-2, 0), (2, 0), (-4, 0), (4, 0), (0, 2)]
 NEAR = [(dx, dy) for dx in range(1, 5) for dy in range(1, 5)]
 CORNER_BC = [(f, dx, dy) for f in (0, 1) for dx, dy in NEAR if dx + dy <= 5 - f]
 CORNER_S = [(0, dx, dy) for dx, dy in NEAR if dx + dy <= 4]
@@ -268,10 +268,13 @@
         lax.fori_loop(0, 8, body, 0)
 
     def pack_fifth(field, packed):
-        for x in range(16):
+        def body(x, _):
             for t in range(4):
-                packed[0, t, x:x + 1, :] = field[6 + x, t, 12:13, :]
-                packed[1, t, x:x + 1, :] = field[6 + x, t, 35:36, :]
+                packed[0, t, pl.ds(x, 1), :] = field[6 + x, t, 12:13, :]
+                packed[1, t, pl.ds(x, 1), :] = field[6 + x, t, 35:36, :]
+            return 0
+
+        lax.fori_loop(0, 16, body, 0)
 
     def send_planes(field, layers):
         own = pl.ds(8, 32)
@@ -281,22 +284,28 @@
         ]
 
     def pack_corners(fields, rows, packed):
-        for cw in (0, 1):
-            for cn in (0, 1):
-                for r, (f, dx, dy) in enumerate(rows):
-                    x = 22 - dx if cw else 5 + dx
-                    y = 40 - dy if cn else 7 + dy
-                    for t in range(4):
-                        packed[2 * cw + cn, t, r:r + 1, :] = fields[f][x, t, y:y + 1, :]
+        def body(corner, _):
+            cw, cn = corner // 2, corner % 2
+            for r, (f, dx, dy) in enumerate(rows):
+                x = 5 + dx + cw * (17 - 2 * dx)
+                y = 7 + dy + cn * (33 - 2 * dy)
+                for t in range(4):
+                    packed[corner, t, r:r + 1, :] = fields[f][x, t, pl.ds(y, 1), :]
+            return 0
+
+        lax.fori_loop(0, 4, body, 0)
 
     def unpack_corners(fields, rows, got):
-        for cw in (0, 1):
-            for cn in (0, 1):
-                for r, (f, dx, dy) in enumerate(rows):
-                    x = 21 + dx if cw else 6 - dx
-                    y = 39 + dy if cn else 8 - dy
-                    for t in range(4):
-                        fields[f][x, t, y:y + 1, :] = got[2 * cw + cn, t, r:r + 1, :]
+        def body(corner, _):
+            cw, cn = corner // 2, corner % 2
+            for r, (f, dx, dy) in enumerate(rows):
+                x = 6 - dx + cw * (15 + 2 * dx)
+                y = 8 - dy + cn * (31 + 2 * dy)
+                for t in range(4):
+                    fields[f][x, t, pl.ds(y, 1), :] = got[corner, t, r:r + 1, :]
+            return 0
+
+        lax.fori_loop(0, 4, body, 0)
 
     def send_corners(corner, got_corner):
         copies = []
@@ -323,10 +332,13 @@
         lax.fori_loop(0, 8, body, 0)
 
     def unpack_fifth(field, got5):
-        for x in range(16):
+        def body(x, _):
             for t in range(4):
-                field[6 + x, t, 3:4, :] = got5[0, t, x:x + 1, :]
-                field[6 + x, t, 44:45, :] = got5[1, t, x:x + 1, :]
+                field[6 + x, t, 3:4, :] = got5[0, t, pl.ds(x, 1), :]
+                field[6 + x, t, 44:45, :] = got5[1, t, pl.ds(x, 1), :]
+            return 0
+
+        lax.fori_loop(0, 16, body, 0)
 
     loads[0].wait()
     to_split(lambda x, r, a: cf[0, x, 8 * r:8 * r + 8, 128 * a:128 * a + 128], tb)
@@ -343,6 +355,16 @@
     round0_coef += send_rows(pk.at[:, 1], py.at[:, 1])
     pack_corners((tb, tc), CORNER_BC, pkc)
     round0_coef += send_corners(pkc, pc)
+    loads[4].wait()
+    for which in (0, 1):
+        for x in range(4):
+            lc[which, 16 + 4 * core + x, n] = cl[which, x]
+    coef_rows = []
+    for dn in (1, 3, 2):
+        mine = lc.at[:, pl.ds(16 + 4 * core, 4), n]
+        coef_rows.append(remote(mine, mine, 0, dn))
+    everything += coef_rows
+
     loads[2].wait()
     to_split(lambda x, r, a: rhs[x, 8 * r:8 * r + 8, 128 * a:128 * a + 128], ts)
     round0_src = send_planes(ts, 4)
@@ -366,10 +388,6 @@
 
     loads[3].wait()
     lax.fori_loop(0, 8, split_mid, 0)
-    loads[4].wait()
-    for which in (0, 1):
-        for x in range(4):
-            lc[which, 16 + 4 * core + x, n] = take(cl[which, x], place)
 
     def mid_slices(dw, dn, depth=8):
         depth = 8 if dw == 0 else depth
@@ -395,6 +413,15 @@
         planes, rows, planes_there, rows_there = mid_slices(dw, dn, 7)
         mid_coef_copies.append(remote(mt.at[:, planes, :, rows], mt.at[:, planes_there, :, rows_there], dw, dn))
     everything += mid_coef_copies
+
+    landed(coef_rows)
+
+    def send_low_coef(dw, rows):
+        src = lc.at[:, pl.ds(16 + 4 * core, 4), rows]
+        return remote(src, lc.at[:, pl.ds(4 * (4 - dw + core), 4), rows], dw, 0)
+
+    low_coef_near = [send_low_coef(dw, pl.ds(0, 4)) for dw in (-2, 2)]
+    everything += low_coef_near
     unpack(tb, py, 2)
     unpack(tc, py, 1)
     unpack_fifth(tb, py5)
@@ -414,12 +441,6 @@
 
     landed(round0_src)
 
-    coef_rows = []
-    for dn in (1, 3, 2):
-        mine = lc.at[:, pl.ds(16 + 4 * core, 4), n]
-        coef_rows.append(remote(mine, mine, 0, dn))
-    everything += coef_rows
-
     unpack(ts, py, 0)
     unpack_corners((ts,), CORNER_S, pcs)
 
@@ -432,14 +453,6 @@
     lax.fori_loop(2, 26, load_fine, 0)
     fine.start(2, 24)
     fine.half_sweep(1, 3, 22)
-
-    landed(coef_rows)
-    def send_low_coef(dw, rows):
-        src = lc.at[:, pl.ds(16 + 4 * core, 4), rows]
-        return remote(src, lc.at[:, pl.ds(4 * (4 - dw + core), 4), rows], dw, 0)
-
-    low_coef_near = [send_low_coef(dw, pl.ds(0, 4)) for dw in (-2, 2)]
-    everything += low_coef_near
 
     fine.half_sweep(0, 4, 20)
     fine.half_sweep(1, 5, 18)
@@ -480,10 +493,12 @@
     mid.half_sweep(0, 6, 12)
     mid.half_sweep(1, 7, 10)
 
+    natural = 4 * (iota(1) % 32) + iota(1) // 32
+
     def restrict_mid(i, _):
         for (j, t), value in mid.restrict_pair(8 + 2 * i).items():
             lstage[i, pl.ds(j, 8, stride=2), :] = value
-        value = lstage[i, 4:12, :]
+        value = take(lstage[i, 4:12, :], natural)
         s2own[i] = value
         s2g[16 + 4 * core + i, n] = value
         return 0
@@ -503,10 +518,6 @@
             copies.append(copy)
         return copies
 
-    landed(low_coef_near + low_coef_far)
-    low_coef_shared = to_sibling(lambda planes: lc.at[:, planes], range(5))
-    everything += low_coef_shared
-
     round2 = send_low(s2own, lambda slot: s2g.at[pl.ds(4 * slot, 4), n])
     everything += round2
 
@@ -522,6 +533,10 @@
         return 0
 
     lax.fori_loop(0, 4, store_mid, 0)
+    landed(low_coef_near + low_coef_far)
+    low_coef_shared = to_sibling(lambda planes: lc.at[:, planes], range(5))
+    everything += low_coef_shared
+
     mid_copies = send_mid(vt, 8)
     everything += mid_copies
 
@@ -544,7 +559,7 @@
 
     landed(low_coef_shared)
     lane, sub = iota(1), iota(0)
-    par = (lane // 4 + sub) % 2 == 0
+    par = (lane + sub) % 2 == 0
     zero = jnp.zeros((8, 128), F32)
     low_lo = 16 - 4 * (w - core)
     low_hi = low_lo + 4 * NW
@@ -579,8 +594,8 @@
                 below = jnp.where(sub == 0, down(h[k][r - 1]) if r else zero, down(here))
                 above = jnp.where(sub == 7, up(h[k][r + 1]) if r < 3 else zero, up(here))
                 lo_y, hi_y = here + below, here + above
-                lo_z = here + jnp.where(lane == 0, zero, left(here))
-                hi_z = here + jnp.where(lane == 127, zero, right(here))
+                lo_z = here + jnp.where(lane == 0, zero, pltpu.roll(here, 1, 1))
+                hi_z = here + jnp.where(lane == 127, zero, pltpu.roll(here, 127, 1))
                 out_x = lo_x if k == 1 else hi_x
                 diags.append(in_x + out_x + lo_y + hi_y + lo_z + hi_z + lc[1, i + k - 1, r])
                 if r == 0:
@@ -634,7 +649,7 @@
                     total = lsrc[colour, p, r] + coef(0) * other[r] + coef(1) * jnp.where(par, a[r], b[r])
                     total += coef(2) * jnp.where(sub == 0, downs[r - 1], downs[r])
                     total += coef(3) * jnp.where(sub == 7, ups[(r + 1) % 4], ups[r])
-                    total += coef(4) * left(other[r]) + coef(5) * right(other[r])
+                    total += coef(4) * pltpu.roll(other[r], 1, 1) + coef(5) * pltpu.roll(other[r], 127, 1)
                     here[p, r] = total * coef(6)
             return 0
 
@@ -656,13 +671,14 @@
     landed(mid_copies)
 
     def correct_mid(i, _):
-        for j in range(4):
-            coarse = v2t[i, pl.ds(8 * n + 4 + j // 2, 8, stride=2), :]
+        for j in (0, 2):
+            coarse = take(v2t[i, pl.ds(8 * n + 4 + j // 2, 8, stride=2), :], place)
             for half in (0, 1):
-                for t in range(2):
-                    x = 2 * i + half
-                    if (half + j + t) % 2 == 1:
-                        mv1[x, j, t // 2] = vt[x, t, pl.ds(j, 8, stride=4), :] + coarse
+                for jj in (j, j + 1):
+                    for t in range(2):
+                        x = 2 * i + half
+                        if (half + jj + t) % 2 == 1:
+                            mv1[x, jj, t // 2] = vt[x, t, pl.ds(jj, 8, stride=4), :] + coarse
         return 0
 
     lax.fori_loop(0, 12, correct_mid, 0)

time: 88.9 us -> 78.8 us (0.89)
  Pallas kernels: 87.4 us -> 77.3 us
    pallas_call x1, Pallas kernels: 70.3 us -> 64.9 us  [v_cycle(): pl.pallas_call(kernel, out_shape=(shape, shape), in_specs=[hbm] * 4, out_...]
    pallas_call x1, Pallas kernels: 12.1 us -> 7.43 us  [moved(): pl.pallas_call(functools.partial(shift_kernel, k), out_shape=(jax.ShapeDt...]
where the time goes in v4:
time: 78.8 us; the launch traced here: 78.6 us
  Pallas kernels  77.3 us (98%)
  between operations  1.29 us (2%)
    pallas_call x1, Pallas kernels, v_cycle(): pl.pallas_call(kernel, out_shape=(shape, shape), in_specs=[hbm] * 4, out_...  64.9 us
    pallas_call x1, Pallas kernels, moved(): pl.pallas_call(functools.partial(shift_kernel, k), out_shape=(jax.ShapeDt...  7.43 us
    pallas_call x1, Pallas kernels, join(): pl.pallas_call(join_kernel, grid=(2,), out_shape=(shape, shape), in_specs...  4.95 us

profile of v4, /device:TPU:1, one launch (start us, length us, event | category | flops | bytes accessed | tf_op | source)
XLA Modules:
  0.0 78.6 jit_solution(13875019078510453182)
XLA Ops:
  1.3 7.5 %conditional.1 = ((f32[2,8,16,256]{3,2,1,0:T(8,128)S(1)}, f32[2,4,8,128]{3,2,1,0:T(8,128)S(1)})) conditional(s32[]{:T(128)} %bitcast, (f32[2,8,16,256]{3,2,1,0:T(8,128)}, f32[2,4,8,128]{3,2,1,0:T(8,128)}) %tuple.100, (f32[2,8,16,256]{3,2,1,0:T(8,128)}, f32[2,4,8,128]{3,2,1,0:T(8,128)}) %tuple.100, ...), branch_computations={%region_0.0_spmd, %region_1.0_spmd, %region_2.0_spmd, %region_3.0_... | conditional | bytes 8 | solution.py:847
  1.3 7.4 %branch_0_fun.1 = (f32[2,8,16,256]{3,2,1,0:T(8,128)S(1)}, f32[2,4,8,128]{3,2,1,0:T(8,128)S(1)}) custom-call(f32[2,8,16,256]{3,2,1,0:T(8,128)} %get-tuple-element.124.cm, f32[2,4,8,128]{3,2,1,0:T(8,128)} %get-tuple-element.125.cl), custom_call_target="tpu_custom_call" | custom-call | tf_op jit(solution)/shard_map/cond/branch_0_fun/pallas_call | solution.py:838
  8.8 64.9 %shard_map.68 = (f32[16,4,32,128]{3,2,1,0:T(8,128)}, f32[16,4,32,128]{3,2,1,0:T(8,128)}) custom-call(f32[16,32,512]{2,1,0:T(8,128)} %rhs_hbm.1, f32[2,16,32,512]{3,2,1,0:T(8,128)} %cf_hbm.1, f32[2,8,16,256]{3,2,1,0:T(8,128)S(1)} %get-tuple-element.192.cm_hbm, f32[2,4,8,128]{3,2,1,0:T(8,128)S(1)} %get-tuple-element.193.cl_hbm), custom_call_target="tpu_custom_call" | custom-call | tf_op jit(solution)/shard_map/pallas_call | solution.py:809
  73.7 5.0 %shard_map.69 = (f32[16,32,512]{2,1,0:T(8,128)}, f32[16,32,512]{2,1,0:T(8,128)}) custom-call(f32[16,4,32,128]{3,2,1,0:T(8,128)} %get-tuple-element.194.v_ref, f32[16,4,32,128]{3,2,1,0:T(8,128)} %get-tuple-element.195.r_ref), custom_call_target="tpu_custom_call" | custom-call | tf_op jit(solution)/shard_map/pallas_call | solution.py:770

commit v5 on v4

--- a/solution.py
+++ b/solution.py
@@ -140,14 +140,18 @@
 
         lax.fori_loop(first, first + count, build, 0, unroll=self.unroll(count))
 
-    def pulled(self, x, j, t, colour, get):
-        J, T, other = self.J, self.T, self.v[1 - colour]
-        total = self.fx[x, j, t] * other[x - 1, j, t // 2] + self.fx[x + 1, j, t] * other[x + 1, j, t // 2]
+    def pulled(self, x, j, t, planes):
+        J, T = self.J, self.T
+        get = planes[1]
+        total = self.fx[x, j, t] * planes[0](j, t) + self.fx[x + 1, j, t] * planes[2](j, t)
         total += self.fy[x, j, t] * (get(j - 1, t) if j else down(get(J - 1, t)))
         total += self.fy[x, j + 1, t] * (get(j + 1, t) if j < J - 1 else up(get(0, t)))
         total += self.fz[x, j, t] * (get(j, t - 1) if t else left(get(j, T - 1)))
         total += self.fz[x, j, t + 1] * (get(j, t + 1) if t < T - 1 else right(get(j, 0)))
         return total
+
+    def readers(self, x, parity):
+        return [self.reader(x + k, (parity + k) % 2) for k in (-1, 0, 1, 2)]
 
     def reader(self, x, parity):
         seen = {}
@@ -171,27 +175,26 @@
 
     def half_sweep(self, colour, first, count):
         def body(i, _):
+            planes = self.readers(first + 2 * i, first % 2)
             for half in (0, 1):
                 x = first + 2 * i + half
-                get = self.reader(x, (first + half) % 2)
                 for j, t in self.cells((first + half + colour) % 2):
-                    total = self.src[x, j, t] + self.pulled(x, j, t, colour, get)
+                    total = self.src[x, j, t] + self.pulled(x, j, t, planes[half:half + 3])
                     self.v[colour][x, j, t // 2] = total * self.rinv[x, j, t]
             return 0
 
         lax.fori_loop(0, count // 2, body, 0, unroll=self.unroll(count // 2))
 
-    def residual(self, x, parity, j, t, get):
-        pulled = self.pulled(x, j, t, (parity + j + t) % 2, get)
-        return self.src[x, j, t] - (self.diag[x, j, t] * get(j, t) - pulled)
+    def residual(self, x, j, t, planes):
+        return self.src[x, j, t] - (self.diag[x, j, t] * planes[1](j, t) - self.pulled(x, j, t, planes))
 
     def restrict_pair(self, x):
         sums = {}
+        planes = self.readers(x, 0)
         for half in (0, 1):
-            get = self.reader(x + half, half)
             for j in range(self.J):
                 for t in range(self.T):
-                    value = self.residual(x + half, half, j, t, get)
+                    value = self.residual(x + half, j, t, planes[half:half + 3])
                     key = (j // 2, t // 2)
                     sums[key] = sums[key] + value if key in sums else value
         return {key: 0.5 * value for key, value in sums.items()}
@@ -343,16 +346,16 @@
     loads[0].wait()
     to_split(lambda x, r, a: cf[0, x, 8 * r:8 * r + 8, 128 * a:128 * a + 128], tb)
     pl.semaphore_wait(barrier, len(GREETED))
-    round0_coef = send_planes(tb, 5)
     pack(tb, pk, 2)
-    round0_coef += send_rows(pk.at[:, 2], py.at[:, 2])
+    round0_coef = send_rows(pk.at[:, 2], py.at[:, 2])
+    round0_coef += send_planes(tb, 5)
     pack_fifth(tb, pk5)
     round0_coef += send_rows(pk5, py5)
     loads[1].wait()
     to_split(lambda x, r, a: cf[1, x, 8 * r:8 * r + 8, 128 * a:128 * a + 128], tc)
-    round0_coef += send_planes(tc, 4)
     pack(tc, pk, 1)
     round0_coef += send_rows(pk.at[:, 1], py.at[:, 1])
+    round0_coef += send_planes(tc, 4)
     pack_corners((tb, tc), CORNER_BC, pkc)
     round0_coef += send_corners(pkc, pc)
     loads[4].wait()
@@ -367,9 +370,9 @@
 
     loads[2].wait()
     to_split(lambda x, r, a: rhs[x, 8 * r:8 * r + 8, 128 * a:128 * a + 128], ts)
-    round0_src = send_planes(ts, 4)
     pack(ts, pk, 0)
-    round0_src += send_rows(pk.at[:, 0], py.at[:, 0])
+    round0_src = send_rows(pk.at[:, 0], py.at[:, 0])
+    round0_src += send_planes(ts, 4)
     pack_corners((ts,), CORNER_S, pkcs)
     round0_src += send_corners(pkcs, pcs)
     round0 = round0_coef + round0_src
@@ -421,7 +424,8 @@
         return remote(src, lc.at[:, pl.ds(4 * (4 - dw + core), 4), rows], dw, 0)
 
     low_coef_near = [send_low_coef(dw, pl.ds(0, 4)) for dw in (-2, 2)]
-    everything += low_coef_near
+    low_coef_far = [send_low_coef(dw, pl.ds(n // 2, 3)) for dw in (-4, 4)]
+    everything += low_coef_near + low_coef_far
     unpack(tb, py, 2)
     unpack(tc, py, 1)
     unpack_fifth(tb, py5)
@@ -444,14 +448,18 @@
     unpack(ts, py, 0)
     unpack_corners((ts,), CORNER_S, pcs)
 
-    def load_fine(x, _):
-        for j in range(6):
-            for t in range(4):
-                fsrc[x, j, t] = ts[x, t, pl.ds(j, 8, stride=6), :]
-        return 0
-
-    lax.fori_loop(2, 26, load_fine, 0)
-    fine.start(2, 24)
+    def load_fine(q, _):
+        for half in (0, 1):
+            x = 2 + 2 * q + half
+            for j in range(6):
+                for t in range(4):
+                    value = ts[x, t, pl.ds(j, 8, stride=6), :]
+                    fsrc[x, j, t] = value
+                    if (half + j + t) % 2 == 0:
+                        fv0[x, j, t // 2] = value * frinv[x, j, t]
+        return 0
+
+    lax.fori_loop(0, 12, load_fine, 0)
     fine.half_sweep(1, 3, 22)
 
     fine.half_sweep(0, 4, 20)
@@ -467,8 +475,7 @@
     lax.fori_loop(0, 8, restrict_fine, 0)
 
     round1 = send_mid(st, 6)
-    low_coef_far = [send_low_coef(dw, pl.ds(n // 2, 3)) for dw in (-4, 4)]
-    everything += round1 + low_coef_far
+    everything += round1
 
     landed(mid_coef_copies)
     mid = Level(4, 2, mh, mfx, mfy, mfz, mrinv, mdiag, msrc, (mv0, mv1))
@@ -729,13 +736,13 @@
         return pltpu.make_async_copy(staged.at[6 + x, :, pl.ds(8, 32)], hbm.at[x], out_sem.at[k, x])
 
     def finish(q, _):
+        planes = fine.readers(6 + 2 * q, 0)
         for half in (0, 1):
             x = 2 * q + half
-            get = fine.reader(6 + x, half)
             for j in range(6):
                 for t in range(4):
-                    ts[6 + x, t, pl.ds(j, 8, stride=6), :] = get(j, t)
-                    tc[6 + x, t, pl.ds(j, 8, stride=6), :] = fine.residual(6 + x, half, j, t, get)
+                    ts[6 + x, t, pl.ds(j, 8, stride=6), :] = planes[1 + half](j, t)
+                    tc[6 + x, t, pl.ds(j, 8, stride=6), :] = fine.residual(6 + x, j, t, planes[half:half + 3])
             result(0, x).start()
             result(1, x).start()
         return 0

time: 78.8 us -> 80.4 us (1.020); the launches traced: 78.6 us -> 79.2 us
    pallas_call x1, Pallas kernels: 7.43 us -> 9.94 us  [moved(): pl.pallas_call(functools.partial(shift_kernel, k), out_shape=(jax.ShapeDt...]
    pallas_call x1, Pallas kernels: 64.9 us -> 63 us  [v_cycle(): pl.pallas_call(kernel, out_shape=(shape, shape), in_specs=[hbm] * 4, out_...]
where the time goes in v5:
time: 80.4 us; the launch traced here: 79.2 us
  Pallas kernels  77.9 us (97%)
  between operations  1.29 us (2%)
    pallas_call x1, Pallas kernels, v_cycle(): pl.pallas_call(kernel, out_shape=(shape, shape), in_specs=[hbm] * 4, out_...  63 us
    pallas_call x1, Pallas kernels, moved(): pl.pallas_call(functools.partial(shift_kernel, k), out_shape=(jax.ShapeDt...  9.94 us
    pallas_call x1, Pallas kernels, join(): pl.pallas_call(join_kernel, grid=(2,), out_shape=(shape, shape), in_specs...  4.95 us

profile of v5, /device:TPU:1, one launch (start us, length us, event | category | flops | bytes accessed | tf_op | source)
XLA Modules:
  0.0 79.2 jit_solution(3680064300874227598)
XLA Ops:
  1.3 10.0 %conditional.1 = ((f32[2,8,16,256]{3,2,1,0:T(8,128)S(1)}, f32[2,4,8,128]{3,2,1,0:T(8,128)S(1)})) conditional(s32[]{:T(128)} %bitcast, (f32[2,8,16,256]{3,2,1,0:T(8,128)}, f32[2,4,8,128]{3,2,1,0:T(8,128)}) %tuple.100, (f32[2,8,16,256]{3,2,1,0:T(8,128)}, f32[2,4,8,128]{3,2,1,0:T(8,128)}) %tuple.100, ...), branch_computations={%region_0.0_spmd, %region_1.0_spmd, %region_2.0_spmd, %region_3.0_... | conditional | bytes 8 | solution.py:854
  1.3 9.9 %branch_23_fun.1 = (f32[2,8,16,256]{3,2,1,0:T(8,128)S(1)}, f32[2,4,8,128]{3,2,1,0:T(8,128)S(1)}) custom-call(f32[2,8,16,256]{3,2,1,0:T(8,128)} %get-tuple-element.170.cm, f32[2,4,8,128]{3,2,1,0:T(8,128)} %get-tuple-element.171.cl), custom_call_target="tpu_custom_call" | custom-call | tf_op jit(solution)/shard_map/cond/branch_23_fun/pallas_call | solution.py:845
  11.3 63.0 %shard_map.68 = (f32[16,4,32,128]{3,2,1,0:T(8,128)}, f32[16,4,32,128]{3,2,1,0:T(8,128)}) custom-call(f32[16,32,512]{2,1,0:T(8,128)} %rhs_hbm.1, f32[2,16,32,512]{3,2,1,0:T(8,128)} %cf_hbm.1, f32[2,8,16,256]{3,2,1,0:T(8,128)S(1)} %get-tuple-element.192.cm_hbm, f32[2,4,8,128]{3,2,1,0:T(8,128)S(1)} %get-tuple-element.193.cl_hbm), custom_call_target="tpu_custom_call" | custom-call | tf_op jit(solution)/shard_map/pallas_call | solution.py:816
  74.3 5.0 %shard_map.69 = (f32[16,32,512]{2,1,0:T(8,128)}, f32[16,32,512]{2,1,0:T(8,128)}) custom-call(f32[16,4,32,128]{3,2,1,0:T(8,128)} %get-tuple-element.194.v_ref, f32[16,4,32,128]{3,2,1,0:T(8,128)} %get-tuple-element.195.r_ref), custom_call_target="tpu_custom_call" | custom-call | tf_op jit(solution)/shard_map/pallas_call | solution.py:777
